TPU v7x, 256 devices: a whole 4x4x8 slice. The times are simulated.
256 devices in a mesh: dp: 32 (over z, x), mp: 4 (over y), helper: 2 (over core).
Axes of the slice: x: 4, y: 4, z: 8, core: 2. Of those that a mesh axis runs over, the one named last changes fastest.
Arguments:
- activations: bfloat16 [4096, 2048], P('dp', ('mp', 'helper')), may hold values from -64 to 64
- output_grads: bfloat16 [4096, 16384], P('dp'), may hold values from -0.4375 to 0.4375
- left_state: float32 [4, 32, 512, 512], P('mp', 'dp', 'helper'), may hold values from -6 to 368640, as said below
- right_state: float32 [4, 32, 512, 512], P('mp', 'dp', 'helper'), may hold values from -6 to 122880, as said below
- left_root_old: bfloat16 [4, 32, 512, 512], P('mp', 'dp', 'helper'), may hold values from -0.00021 to 0.1205, as said below
- right_root_old: bfloat16 [4, 32, 512, 512], P('mp', 'dp'), may hold values from -0.00021 to 0.1205, as said below
- refresh: int32 [4, 32], P('mp', 'dp'), may hold values 0 or 1
Outputs:
- update: bfloat16 [4, 2, 256, 16384], P(None, 'helper', None, 'dp')
- left_new: float32 [4, 32, 512, 512], P('mp', 'dp', 'helper')
- right_new: float32 [4, 32, 512, 512], P('mp', 'dp', 'helper')
Inputs may be any that keep to these rules, and one draw needn't show every extreme that they name: `left_state`: symmetric positive definite in each block. `right_state`: symmetric positive definite in each block. `left_root_old`: symmetric in each block. `right_root_old`: symmetric in each block.
All inputs are finite; a program needn't handle non-finite values. No bound on the sum of `refresh` on one device may be relied on, other than what follows from the above.
Results may differ from a plain program's by a relative error of at most 0.024.
Values may be sent and summed in bfloat16 or wider, within the bound.
A program may use at most 64 MiB of HBM per device.

v0:
```python
import jax
import jax.numpy as jnp
from jax import lax
from jax.sharding import PartitionSpec as P

decay_rate = 0.95
epsilon = 1e-06


def inverse_root(matrix):
    highest = lax.Precision.HIGHEST
    order = matrix.shape[0]
    identity = jnp.eye(order, dtype=matrix.dtype)
    scale = order * jnp.sqrt(jnp.mean(matrix * matrix) + epsilon)
    current = matrix / scale
    factor = (5.0 * identity - current) / 4.0
    result = factor * lax.rsqrt(jnp.sqrt(scale))
    square = jnp.dot(factor, factor, precision=highest)
    quartic = jnp.dot(square, square, precision=highest)
    current = jnp.dot(quartic, current, precision=highest)
    factor = (5.0 * identity - current) / 4.0
    result = jnp.dot(result, factor, precision=highest)
    return result


def shards(
    activations, output_grads, left_state, right_state, left_root_old, right_root_old, refresh
):
    highest = lax.Precision.HIGHEST
    piece_rows = left_state.shape[2]
    block_width = left_state.shape[3]
    tokens = activations.shape[0]
    helper_place = lax.axis_index("helper")
    column_blocks = output_grads.reshape(tokens, -1, block_width)
    product = jnp.einsum(
        "tq,tnc->nqc", activations, column_blocks, preferred_element_type=jnp.float32
    )
    grad_piece = lax.psum_scatter(
        product.reshape(lax.axis_size("dp") * piece_rows, block_width).astype(jnp.bfloat16),
        "dp",
        scatter_dimension=0,
        tiled=True,
    ).astype(jnp.float32)
    old_left = left_state[0, 0]
    old_right = right_state[0, 0]
    grad_full = lax.all_gather(
        grad_piece.astype(jnp.bfloat16), "helper", axis=0, tiled=True
    ).astype(grad_piece.dtype)
    own_columns = lax.dynamic_slice_in_dim(grad_full, helper_place * piece_rows, piece_rows, 1)
    left_rows = decay_rate * old_left + jnp.dot(grad_piece, grad_full.T, precision=highest)
    right_rows = decay_rate * old_right + jnp.dot(own_columns.T, grad_full, precision=highest)
    full_left, full_right = (
        lax.all_gather(left_rows.astype(jnp.bfloat16), "helper", axis=0, tiled=True).astype(
            left_rows.dtype
        ),
        lax.all_gather(right_rows.astype(jnp.bfloat16), "helper", axis=0, tiled=True).astype(
            right_rows.dtype
        ),
    )
    fresh_flag = refresh[0, 0] > 0

    def renew():
        left_whole = inverse_root(full_left).astype(jnp.bfloat16)
        return (
            lax.dynamic_slice_in_dim(left_whole, helper_place * piece_rows, piece_rows, 0),
            inverse_root(full_right).astype(jnp.bfloat16),
        )

    def keep_old():
        return (left_root_old[0, 0], right_root_old[0, 0])

    left_root, right_root = lax.cond(fresh_flag, renew, keep_old)
    grad_half = grad_full.astype(jnp.bfloat16)
    half_product = jnp.dot(left_root, grad_half, preferred_element_type=jnp.float32).astype(
        jnp.bfloat16
    )
    shaped = jnp.dot(half_product, right_root, preferred_element_type=jnp.float32)
    totals = lax.psum((jnp.sum(grad_piece * grad_piece), jnp.sum(shaped * shaped)), "helper")
    entries = block_width * block_width
    graft_ratio = jnp.sqrt(totals[0] / entries + epsilon) / jnp.sqrt(totals[1] / entries + epsilon)
    scaled = (graft_ratio * shaped).astype(jnp.bfloat16)
    gathered = lax.all_gather(scaled[None, None], "mp", axis=0, tiled=True)
    return (gathered, left_rows[None, None], right_rows[None, None])


def solution(mesh):
    placed = (
        P("dp", ("mp", "helper")),
        P("dp", None),
        P("mp", "dp", "helper", None),
        P("mp", "dp", "helper", None),
        P("mp", "dp", "helper", None),
        P("mp", "dp", None, None),
        P("mp", "dp"),
    )
    return jax.shard_map(
        shards,
        mesh=mesh,
        in_specs=placed,
        out_specs=(
            P(None, "helper", None, "dp"),
            P("mp", "dp", "helper", None),
            P("mp", "dp", "helper", None),
        ),
        check_vma=False,
    )
```

profile of v0, /device:TPU:1, one launch (start us, length us, event | category | flops | bytes accessed | tf_op | source)
XLA Modules:
  0.0 324.4 jit_solution(2049411131759916742)
XLA Ops:
  7.2 0.0 copy-start
  7.2 0.0 reduce-scatter.2.cloned.1.call-start
  7.2 1.7 copy.32
  8.9 0.0 copy-done
  8.9 7.8 %convolution_convert_fusion.1 = bf16[32,512,256]{1,2,0:T(8,128)(2,1)} fusion(bf16[16,32,8,512]{3,2,1,0:T(8,128)(2,1)} %bitcast.37, bf16[128,256]{1,0:T(8,128)(2,1)S(1)} %copy-done), kind=kOutput, calls=%fused_computation.42 | convolution fusion | flops 1077936128 | bytes 12648448 | tf_op jit(solution)/shard_map/tq,tnc->nqc/dot_general | solution.py:35
  16.7 0.0 copy-start.3
  16.7 0.0 reduce-scatter.2.cloned.1.call-update
  16.7 0.0 all-gather.3.cloned.1.call-start
  17.5 228.4 %reduce-scatter.2.cloned.1.call-done = bf16[256,512]{1,0:T(8,128)(2,1)} async-done(((bf16[8192,512]{1,0:T(8,128)(2,1)}), bf16[256,512]{1,0:T(8,128)(2,1)}) %reduce-scatter.2.cloned.1.call-update) | async-done | bytes 262160 | tf_op jit(solution)/shard_map/reduce_scatter | solution.py:38
  245.9 0.0 copy-start.1
  245.9 6.7 %all_gather.12 = bf16[512,512]{1,0:T(8,128)(2,1)S(1)} all-gather(bf16[256,512]{1,0:T(8,128)(2,1)} %reduce-scatter.2.cloned.1.call-done), channel_id=1, replica_groups=mesh['dp'=32,'mp'=4,'helper'=2] {'helper'}, dimensions={0}, use_global_device_ids=true | all-gather | bytes 786432 | tf_op jit(solution)/shard_map/all_gather | solution.py:46
  252.6 0.0 copy-done.3
  252.6 0.0 copy-start.2
  252.6 1.1 fusion.38
  253.7 2.2 all_gather.14
  255.9 0.1 convert_element_type.56
  256.0 0.0 copy-done.1
  256.0 2.2 fusion.37
  258.2 2.2 all_gather.13
  260.3 0.1 convert_element_type.54
  260.5 0.0 copy-done.2
  260.5 0.2 conditional.1
  260.7 2.1 multiply_reduce_fusion.2
  262.8 0.7 multiply_reduce_fusion.3
  263.6 3.1 all-reduce
  268.0 0.7 multiply_convert_fusion
  268.7 0.0 all-gather.3.cloned.1.call-update
  268.7 46.5 %all-gather.3.cloned.1.call-done = bf16[1024,512]{1,0:T(8,128)(2,1)} async-done(((bf16[256,512]{1,0:T(8,128)(2,1)}), bf16[1024,512]{1,0:T(8,128)(2,1)}) %all-gather.3.cloned.1.call-update) | async-done | bytes 1048592 | tf_op jit(solution)/shard_map/all_gather | solution.py:82
  315.3 2.3 copy.34
Async XLA Ops:
  7.2 1.8 copy-start
  7.2 238.7 %reduce-scatter.2.cloned.1.call-start = ((), (), s32[]{:S(2)}) async-start(), calls=%async_computation.1 | async-start | bytes 8650752 | tf_op jit(solution)/shard_map/reduce_scatter | solution.py:38
  16.7 235.8 %copy-start.3 = (f32[1,1,256,512]{3,2,1,0:T(8,128)S(1)}, f32[1,1,256,512]{3,2,1,0:T(8,128)}, u32[]{:S(2)}) copy-start(f32[1,1,256,512]{3,2,1,0:T(8,128)} %param.12) | copy-start | bytes 1572868
  16.7 298.5 %all-gather.3.cloned.1.call-start = ((), (), s32[]{:S(2)}) async-start(), calls=%async_computation.2 | async-start | bytes 1310720 | tf_op jit(solution)/shard_map/all_gather | solution.py:82
  245.9 10.1 %copy-start.1 = (bf16[256,512]{1,0:T(8,128)(2,1)S(1)}, bf16[256,512]{1,0:T(8,128)(2,1)}, u32[]{:S(2)}) copy-start(bf16[256,512]{1,0:T(8,128)(2,1)} %reduce-scatter.2.cloned.1.call-done) | copy-start | bytes 786436
  252.6 7.9 %copy-start.2 = (bf16[1,1,512,512]{3,2,1,0:T(8,128)(2,1)S(1)}, bf16[1,1,512,512]{3,2,1,0:T(8,128)(2,1)}, u32[]{:S(2)}) copy-start(bf16[1,1,512,512]{3,2,1,0:T(8,128)(2,1)} %param.14) | copy-start | bytes 1572868
Sparse Core Ops, SparseCore 0:
  16.9 228.9 reduce-scatter.1
  268.9 46.3 all-gather.2
where the time goes:
time: 325 us; the launch traced here: 324 us
  waiting for transfers between devices  275 us (85%)
  between operations  16.1 us (5%)
  blocking collectives  14.1 us (4%)
  matrix products  13.2 us (4%)
  local copies, waits for them, and re-layouts  3.98 us (1%)
    reduce_scatter x1, waiting for transfers between devices, shards(): lax.psum_scatter(product.reshape(lax.axis_size('dp') * piece_rows, block_...  228 us
    all_gather x1, waiting for transfers between devices, shards(): gathered = lax.all_gather(scaled[None, None], 'mp', axis=0, tiled=True)  46.5 us
    dot_general x1, matrix products, shards(): jnp.einsum('tq,tnc->nqc', activations, column_blocks, preferred_element_t...  7.78 us
    all_gather x1, blocking collectives, shards(): lax.all_gather(grad_piece.astype(jnp.bfloat16), 'helper', axis=0, tiled=T...  6.7 us
  transfers between devices with their start and end apart: 2, of which 2 were waited for; matrix products, arithmetic and copies ran while one was open for 0% of the time, Pallas kernels for 0%

commit v1 on v0

v1 whole, which is shorter than its diff:
```python
import jax
import jax.numpy as jnp
from jax import lax
from jax.experimental import pallas as pl
from jax.experimental.pallas import tpu as pltpu
from jax.sharding import PartitionSpec as P

decay_rate = 0.95
epsilon = 1e-06

NZ, NX, NY = 8, 4, 4
BLK = 512
PIECE = 256
TOKENS = 128
ROWS = 16
ORDER = (0, 1, 7, 2, 6, 3, 5, 4)
SLOT = {distance: slot for slot, distance in enumerate(ORDER)}
STAGES = ((0, 0, 8), (1, 0, 8), (2, 0, 8), (3, 0, 4), (3, 4, 8))
VMEM_LIMIT = 56 * 2**20
MESH = pl.DeviceIdType.MESH


def place():
    d = lax.axis_index("dp")
    return d // NX, d % NX, lax.axis_index("mp"), lax.axis_index("helper")


def remote(src, dst, send, recv, device):
    return pltpu.make_async_remote_copy(
        src_ref=src,
        dst_ref=dst,
        send_sem=send,
        recv_sem=recv,
        device_id=device,
        device_id_type=MESH,
    )


def across_rows(a, b):
    return lax.dot_general(a, b, (((0,), (0,)), ((), ())), preferred_element_type=jnp.float32)


def inverse_root(s):
    b16 = jnp.bfloat16
    scale = BLK * jnp.sqrt(jnp.sum(s * s) * (1.0 / (BLK * BLK)) + epsilon)
    first = s * (1.0 / scale)
    first16 = first.astype(b16)
    second = jnp.dot(first16, first16, preferred_element_type=jnp.float32)
    third = jnp.dot(second.astype(b16), first16, preferred_element_type=jnp.float32)
    upper = (250.0 / 4096) * first - (25.0 / 4096) * second + (1.0 / 4096) * third
    high = jnp.dot(third.astype(b16), upper.astype(b16), preferred_element_type=jnp.float32)
    rows = lax.broadcasted_iota(jnp.int32, s.shape, 0)
    columns = lax.broadcasted_iota(jnp.int32, s.shape, 1)
    constant = jnp.where(rows == columns, 25.0 / 16, 0.0)
    low = (-5.0 / 16 - 3125.0 / 4096) * first + (3125.0 / 4096) * second - (1250.0 / 4096) * third
    return ((constant + low + high) * lax.rsqrt(jnp.sqrt(scale))).astype(b16)


def step_kernel(
    fresh,
    act_ref,
    og_ref,
    left_ref,
    right_ref,
    lroot_ref,
    rroot_ref,
    out,
    left_new,
    right_new,
    act_buf,
    act_t,
    act_other,
    act_t2,
    og_buf,
    q_buf,
    stats,
    lroot,
    rroot,
    piece,
    shaped,
    total,
    part_out,
    part_in,
    own_sem,
    z_send,
    z_recv,
    a_send,
    a_recv,
    x_send,
    x_recv,
    y_send,
    y_recv,
    c_send,
    c_recv,
    r_send,
    r_recv,
    s_send,
    s_recv,
    u_send,
    u_recv,
    out_sem,
):
    z, x, y, h = place()

    g = y * 2 + h

    pair = x + 1 - 2 * lax.rem(x, 2)
    partner = NX - 1 - x

    def at(dz, column=x):
        return (lax.rem(z + dz, NZ) * NX + column, y, h)

    def at_y(k):
        return (z * NX + x, lax.rem(y + k, NY), h)

    sibling = (z * NX + x, y, 1 - h)
    barrier = pltpu.get_barrier_semaphore()
    peers = [at(dz) for dz in range(1, NZ)] + [at(dz, pair) for dz in range(NZ)]
    peers += [at(0, partner), at_y(1), at_y(3), sibling]
    for peer in peers:
        pl.semaphore_signal(barrier, inc=1, device_id=peer, device_id_type=MESH)

    def start(copies):
        for copy in copies:
            copy.start()

    def await_bytes(ref, sem):
        pltpu.make_async_copy(ref, ref, sem).wait()

    here = pl.ds(pl.multiple_of(h * PIECE, PIECE), PIECE)
    there = pl.ds(pl.multiple_of((1 - h) * PIECE, PIECE), PIECE)

    def target(c):
        owner = pair if c % 2 else x
        return owner, (owner if c >= 2 else NX - 1 - owner)

    def og_part(dz, c):
        column = (lax.rem(z + dz, NZ) * NX + target(c)[1]) * BLK
        return og_ref.at[
            pl.ds(pl.multiple_of(g * ROWS, ROWS), ROWS), pl.ds(pl.multiple_of(column, BLK), BLK)
        ]

    own_og = [
        pltpu.make_async_copy(og_part(0, c), og_buf.at[c, 0, y, h], own_sem.at[c * 3])
        for c in (0, 2)
    ]
    own_act = pltpu.make_async_copy(act_ref, act_buf.at[0, 0], own_sem.at[1])
    start(own_og + [own_act])
    pl.semaphore_wait(barrier, len(peers))

    def send_og(i):
        c, first, end = STAGES[i]
        for slot in reversed(range(first, end)):
            if slot or c % 2:
                remote(
                    og_part(ORDER[slot], c),
                    og_buf.at[c, slot, y, h],
                    z_send.at[i],
                    z_recv.at[i],
                    at(ORDER[slot], target(c)[0]),
                ).start()

    def og_bytes(i):
        c, first, end = STAGES[i]
        return og_buf.at[c, first if c % 2 else first + 1 : end, 0, 0]

    def act_at(bank, distance, rows=slice(None)):
        return act_buf.at[bank, SLOT[distance % NZ], rows]

    def send_act(i):
        if i < 4:
            rows_up, rows_down = (slice(0, 2), slice(2, 4)) if i == 3 else (slice(None),) * 2
            up = act_at(0, i, rows_up) if i else act_ref
            down = act_at(0, -i, rows_down) if i else act_ref
            start(
                [
                    remote(up, act_at(0, i + 1, rows_up), a_send, a_recv.at[i], at(1)),
                    remote(down, act_at(0, -i - 1, rows_down), a_send, a_recv.at[i], at(7)),
                ]
            )
        for distance in (i, -i) if 0 < i < 4 else (i,):
            src = act_at(0, distance) if i else act_ref
            remote(src, act_at(1, distance), x_send, x_recv, at(0, pair)).start()

    def next_act(i):
        await_bytes(act_buf.at[0, 0:2] if i < 4 else act_buf.at[0, 0], a_recv.at[i - 1])
        send_act(i)

    low, high, far = lax.rem(y + 3, NY), lax.rem(y + 1, NY), lax.rem(y + 2, NY)

    def cross(i, rows):
        c, first, end = STAGES[i]
        if c < 3:
            ref = og_buf.at[c, first:end, rows, h]
            remote(ref, ref, c_send, c_recv.at[c], sibling).start()

    def first_y(i):
        c, first, end = STAGES[i]
        if c % 2 == 0:
            own_og[c // 2].wait()
        await_bytes(og_bytes(i), z_recv.at[i])
        mine = og_buf.at[c, first:end, y, h]
        start(
            [
                remote(mine, mine, y_send, y_recv.at[i, 0], at_y(1)),
                remote(mine, mine, y_send, y_recv.at[i, 0], at_y(3)),
            ]
        )
        cross(i, y)

    def second_y(i):
        c, first, end = STAGES[i]
        await_bytes(og_buf.at[c, first:end, 0:2, 0], y_recv.at[i, 0])
        middle = (first + end) // 2
        up, down = og_buf.at[c, first:middle, low, h], og_buf.at[c, middle:end, high, h]
        start(
            [
                remote(up, up, y_send, y_recv.at[i, 1], at_y(1)),
                remote(down, down, y_send, y_recv.at[i, 1], at_y(3)),
            ]
        )
        cross(i, low)
        cross(i, high)

    def third_y(i):
        c, first, end = STAGES[i]
        await_bytes(og_buf.at[c, first:end, 0, 0], y_recv.at[i, 1])
        cross(i, far)

    def turn(bank):
        act_t[bank] = act_buf[bank].reshape(NZ * TOKENS, PIECE).T

    def product(c):
        await_bytes(og_buf.at[c, :, :, 0], c_recv.at[c])
        rows = og_buf[c].reshape(NZ * TOKENS, BLK)
        part = jnp.dot(act_t[c % 2], rows, preferred_element_type=jnp.float32)
        if c == 1:
            part_out[...] = (total[...] + part).astype(jnp.bfloat16)
        else:
            total[...] = part

    def split_product(i):
        c, first, end = STAGES[i]
        rows = og_buf[c, first:end, :, h].reshape((end - first) * NY * ROWS, BLK)
        columns = act_t2[:, first * NY * ROWS : end * NY * ROWS]
        return jnp.dot(columns, rows, preferred_element_type=jnp.float32)

    olds = [
        pltpu.make_async_copy(left_ref, stats.at[0, here], own_sem.at[2]),
        pltpu.make_async_copy(right_ref, stats.at[1, here], own_sem.at[3]),
        pltpu.make_async_copy(lroot_ref, lroot.at[here], own_sem.at[4]),
        pltpu.make_async_copy(rroot_ref, rroot, own_sem.at[5]),
        remote(left_ref, stats.at[0, here], s_send.at[0], s_recv.at[0], sibling),
        remote(right_ref, stats.at[1, here], s_send.at[1], s_recv.at[1], sibling),
        remote(lroot_ref, lroot.at[here], s_send.at[2], s_recv.at[2], sibling),
    ]
    act_copy = remote(act_buf.at[1, :, :, 1 - h], act_other, s_send.at[4], s_recv.at[4], sibling)
    r_copy = remote(part_out, part_in, r_send, r_recv, at(0, partner))

    send_act(0)
    send_og(0)
    own_act.wait()
    for i in range(4):
        await_bytes(og_bytes(i), z_send.at[i])
        send_og(i + 1)
        next_act(i + 1)
        if i == 0:
            start(olds)
        first_y(i)
        if i >= 1:
            second_y(i - 1)
        if i >= 2:
            third_y(i - 2)
        if i == 3:
            turn(0)
            product(0)
    await_bytes(act_buf.at[1], x_recv)
    act_copy.start()
    first_y(4)
    second_y(3)
    third_y(2)
    turn(1)
    product(1)
    r_copy.start()
    second_y(4)
    third_y(3)
    product(2)
    for copy in olds:
        copy.wait()
    stats[...] = decay_rate * stats[...]
    act_copy.wait()
    act_t2[here] = act_buf[1, :, :, h].reshape(NZ * NY * ROWS, PIECE).T
    act_t2[there] = act_other[...].reshape(NZ * NY * ROWS, PIECE).T
    shaped[...] = split_product(3)
    r_copy.wait_recv()
    shaped[here] = shaped[here] + total[...] + part_in[...].astype(jnp.float32)
    third_y(4)
    shaped[...] = shaped[...] + split_product(4)
    q_buf[0] = shaped[...].astype(jnp.bfloat16)
    q_copy = remote(q_buf.at[0], q_buf.at[1], s_send.at[3], s_recv.at[3], sibling)
    q_copy.start()
    q_copy.wait_recv()
    grad_wide = q_buf[0].astype(jnp.float32) + q_buf[1].astype(jnp.float32)
    grad = grad_wide.astype(jnp.bfloat16)
    grad_square = jnp.sum(grad_wide * grad_wide)
    stats[1] = stats[1] + across_rows(grad, grad)
    right_copy = pltpu.make_async_copy(stats.at[1, here], right_new, out_sem.at[0])
    right_copy.start()
    stats[0] = stats[0] + lax.dot_general(
        grad, grad, (((1,), (1,)), ((), ())), preferred_element_type=jnp.float32
    )
    left_copy = pltpu.make_async_copy(stats.at[0, here], left_new, out_sem.at[1])
    left_copy.start()
    renew = fresh[0, 0] > 0
    lroot[...] = jnp.where(renew, inverse_root(stats[0]), lroot[...])
    rroot[...] = jnp.where(renew, inverse_root(stats[1]), rroot[...])
    half = jnp.dot(lroot[...], grad, preferred_element_type=jnp.float32).astype(jnp.bfloat16)
    shaped[...] = jnp.dot(half, rroot[...], preferred_element_type=jnp.float32)
    entries = 1.0 / (BLK * BLK)
    ratio = jnp.sqrt(grad_square * entries + epsilon) / jnp.sqrt(
        jnp.sum(shaped[...] * shaped[...]) * entries + epsilon
    )
    piece[...] = (ratio * shaped[here]).astype(jnp.bfloat16)

    below, above = lax.rem(y + 3, NY), lax.rem(y + 1, NY)
    bottom, top = pl.ds(0, PIECE // 2), pl.ds(PIECE // 2, PIECE // 2)

    def spread(i, rows, owner, k):
        src = piece.at[rows] if owner is y else out.at[owner, rows]
        return remote(src, out.at[owner, rows], u_send.at[i], u_recv.at[i], at_y(k))

    first = [spread(0, bottom, y, 1), spread(1, top, y, 3)]
    rest = [spread(2, top, y, 1), spread(3, bottom, y, 3)]
    second = [spread(4, bottom, below, 1), spread(5, top, above, 3)]
    start(first + rest)
    own_copy = pltpu.make_async_copy(piece, out.at[y], out_sem.at[2])
    own_copy.start()
    await_bytes(act_buf.at[0, 0 : NZ - 1], a_send)
    await_bytes(act_buf.at[0], x_send)
    await_bytes(og_buf.at[:, :, 0:3, 0], y_send)
    await_bytes(og_buf.at[0:3, :, :, 0], c_send)
    await_bytes(og_bytes(4), z_send.at[4])
    r_copy.wait_send()
    q_copy.wait_send()
    for one, two in zip(first, second):
        one.wait_recv()
        two.start()
    for copy in rest + second:
        copy.wait_recv()
    for copy in first + rest + second:
        copy.wait_send()
    for copy in (right_copy, left_copy, own_copy):
        copy.wait()


def step(fresh, act, og, left, right, lroot, rroot):
    hbm = pl.BlockSpec(memory_space=pl.ANY)
    dma = pltpu.SemaphoreType.DMA
    f32, b16 = jnp.float32, jnp.bfloat16
    return pl.pallas_call(
        step_kernel,
        out_shape=(
            pltpu.VMEM((NY, PIECE, BLK), b16),
            pltpu.VMEM((PIECE, BLK), f32),
            pltpu.VMEM((PIECE, BLK), f32),
        ),
        in_specs=[pl.BlockSpec(memory_space=pltpu.SMEM)] + [hbm] * 6,
        out_specs=(hbm,) * 3,
        scratch_shapes=[
            pltpu.VMEM((2, NZ, NY, 2, ROWS, PIECE), b16),
            pltpu.VMEM((2, PIECE, NZ * TOKENS), b16),
            pltpu.VMEM((NZ, NY, ROWS, PIECE), b16),
            pltpu.VMEM((BLK, NZ * NY * ROWS), b16),
            pltpu.VMEM((NX, NZ, NY, 2, ROWS, BLK), b16),
            pltpu.VMEM((2, BLK, BLK), b16),
            pltpu.VMEM((2, BLK, BLK), f32),
            pltpu.VMEM((BLK, BLK), b16),
            pltpu.VMEM((BLK, BLK), b16),
            pltpu.VMEM((PIECE, BLK), b16),
            pltpu.VMEM((BLK, BLK), f32),
            pltpu.VMEM((PIECE, BLK), f32),
            pltpu.VMEM((PIECE, BLK), b16),
            pltpu.VMEM((PIECE, BLK), b16),
            dma((7,)),
            dma((5,)),
            dma((5,)),
            dma,
            dma((4,)),
            dma,
            dma,
            dma,
            dma((5, 2)),
            dma,
            dma((3,)),
            dma,
            dma,
            dma((5,)),
            dma((5,)),
            dma((6,)),
            dma((6,)),
            dma((3,)),
        ],
        compiler_params=pltpu.CompilerParams(
            collective_id=0, has_side_effects=True, vmem_limit_bytes=VMEM_LIMIT
        ),
        name="step",
    )(fresh, act.reshape(NY, 2, ROWS, PIECE), og, left, right, lroot, rroot)


def finish_kernel(update, left, right, update_out, left_out, right_out, sems):
    copies = [
        pltpu.make_async_copy(update, update_out, sems.at[0]),
        pltpu.make_async_copy(left, left_out, sems.at[1]),
        pltpu.make_async_copy(right, right_out, sems.at[2]),
    ]
    for copy in copies:
        copy.start()
    for copy in copies:
        copy.wait()


def finish(*arrays):
    vmem = pl.BlockSpec(memory_space=pltpu.VMEM)
    anywhere = pl.BlockSpec(memory_space=pl.ANY)
    return pl.pallas_call(
        finish_kernel,
        out_shape=tuple(jax.ShapeDtypeStruct(a.shape, a.dtype) for a in arrays),
        in_specs=[vmem] * 3,
        out_specs=(anywhere,) * 3,
        scratch_shapes=[pltpu.SemaphoreType.DMA((3,))],
        compiler_params=pltpu.CompilerParams(vmem_limit_bytes=4 * 2**20),
        name="finish",
    )(*arrays)


def shards(act, og, left_state, right_state, left_root_old, right_root_old, refresh):
    update, left_new, right_new = finish(
        *step(
            refresh,
            act,
            og,
            left_state[0, 0],
            right_state[0, 0],
            left_root_old[0, 0],
            right_root_old[0, 0],
        )
    )
    return update[:, None], left_new[None, None], right_new[None, None]


def solution(mesh):
    placed = (
        P("dp", ("mp", "helper")),
        P("dp", None),
        P("mp", "dp", "helper", None),
        P("mp", "dp", "helper", None),
        P("mp", "dp", "helper", None),
        P("mp", "dp", None, None),
        P("mp", "dp"),
    )
    return jax.shard_map(
        shards,
        mesh=mesh,
        in_specs=placed,
        out_specs=(
            P(None, "helper", None, "dp"),
            P("mp", "dp", "helper", None),
            P("mp", "dp", "helper", None),
        ),
        check_vma=False,
    )
```

time: 325 us -> 64.2 us (0.20)
  waiting for transfers between devices: 275 us -> 0 us
  Pallas kernels: 0 us -> 62.9 us
  between operations: 16.1 us -> 1.29 us
  blocking collectives: 14.1 us -> 0 us
  matrix products: 13.2 us -> 0 us
  local copies, waits for them, and re-layouts: 3.98 us -> 0 us
    reduce_scatter x1 -> x0, waiting for transfers between devices: 228 us -> none  [shards(): lax.psum_scatter(product.reshape(lax.axis_size('dp') * piece_rows, block_...]
    pallas_call x0 -> x2, Pallas kernels: none -> 62.9 us  [the longest x1 61.5 us: step(): pl.pallas_call(step_kernel, out_shape=(pltpu.VMEM((NY, PIECE, BLK), b16),...]
    all_gather x1 -> x0, waiting for transfers between devices: 46.5 us -> none  [shards(): gathered = lax.all_gather(scaled[None, None], 'mp', axis=0, tiled=True)]
    dot_general x4 -> x0, matrix products: 13.2 us -> none  [the longest x1 7.78 us: shards(): jnp.einsum('tq,tnc->nqc', activations, column_blocks, preferred_element_t...]
    all_gather x3 -> x0, blocking collectives: 11 us -> none  [the longest x1 6.7 us: shards(): lax.all_gather(grad_piece.astype(jnp.bfloat16), 'helper', axis=0, tiled=T...]
    unnamed x10 -> x0, local copies, waits for them, and re-layouts: 3.98 us -> none
  transfers between devices with their start and end apart: 2 -> 0, of which waited for: 2 -> 0; matrix products, arithmetic and copies ran while one was open for 0% -> 0% of each run, Pallas kernels for 0% -> 0%
where the time goes in v1:
time: 64.2 us; the launch traced here: 64.1 us
  Pallas kernels  62.9 us (98%)
  between operations  1.29 us (2%)
    pallas_call x1, Pallas kernels, step(): pl.pallas_call(step_kernel, out_shape=(pltpu.VMEM((NY, PIECE, BLK), b16),...  61.5 us
    pallas_call x1, Pallas kernels, finish(): pl.pallas_call(finish_kernel, out_shape=tuple((jax.ShapeDtypeStruct(a.sha...  1.34 us

profile of v1, /device:TPU:1, one launch (start us, length us, event | category | flops | bytes accessed | tf_op | source)
XLA Modules:
  0.0 64.1 jit_solution(4940501853812529116)
XLA Ops:
  1.3 61.5 %step.1 = (bf16[4,256,512]{2,1,0:T(8,128)(2,1)S(1)}, f32[256,512]{1,0:T(8,128)S(1)}, f32[256,512]{1,0:T(8,128)S(1)}) custom-call(s32[1,1]{1,0:T(1,128)S(6)} %copy.11.fresh, bf16[4,2,16,256]{3,2,1,0:T(8,128)(2,1)} %bitcast.14, bf16[128,16384]{1,0:T(8,128)(2,1)} %og_ref.1, f32[256,512]{1,0:T(8,128)} %bitcast.10, f32[256,512]{1,0:T(8,128)} %bitcast.11, ...), custom_call_target="tpu_custom_call" | custom-call | tf_op jit(solution)/shard_map/step/pallas_call | solution.py:360
  62.8 1.3 %finish.1 = (bf16[4,256,512]{2,1,0:T(8,128)(2,1)}, f32[256,512]{1,0:T(8,128)}, f32[256,512]{1,0:T(8,128)}) custom-call(bf16[4,256,512]{2,1,0:T(8,128)(2,1)S(1)} %get-tuple-element.9.update, f32[256,512]{1,0:T(8,128)S(1)} %get-tuple-element.10.left, f32[256,512]{1,0:T(8,128)S(1)} %get-tuple-element.11.right), custom_call_target="tpu_custom_call" | custom-call | tf_op jit(solution)/shard_map/finish/pallas_call | solution.py:425

commit v2 on v1

--- a/solution.py
+++ b/solution.py
@@ -11,6 +11,7 @@
 NZ, NX, NY = 8, 4, 4
 BLK = 512
 PIECE = 256
+QUARTER = 64
 TOKENS = 128
 ROWS = 16
 ORDER = (0, 1, 7, 2, 6, 3, 5, 4)
@@ -259,10 +260,12 @@
 
     send_act(0)
     send_og(0)
+    send_og(1)
     own_act.wait()
     for i in range(4):
         await_bytes(og_bytes(i), z_send.at[i])
-        send_og(i + 1)
+        if i < 3:
+            send_og(i + 2)
         next_act(i + 1)
         if i == 0:
             start(olds)
@@ -323,16 +326,18 @@
     piece[...] = (ratio * shaped[here]).astype(jnp.bfloat16)
 
     below, above = lax.rem(y + 3, NY), lax.rem(y + 1, NY)
-    bottom, top = pl.ds(0, PIECE // 2), pl.ds(PIECE // 2, PIECE // 2)
-
-    def spread(i, rows, owner, k):
+
+    def spread(i, quarter, owner, k):
+        rows = pl.ds(quarter * QUARTER, QUARTER)
         src = piece.at[rows] if owner is y else out.at[owner, rows]
         return remote(src, out.at[owner, rows], u_send.at[i], u_recv.at[i], at_y(k))
 
-    first = [spread(0, bottom, y, 1), spread(1, top, y, 3)]
-    rest = [spread(2, top, y, 1), spread(3, bottom, y, 3)]
-    second = [spread(4, bottom, below, 1), spread(5, top, above, 3)]
-    start(first + rest)
+    up = [spread(q, q, y, 1) for q in range(4)]
+    down = [spread(4 + q, 3 - q, y, 3) for q in range(4)]
+    onward = [spread(8, 0, below, 1), spread(9, 3, above, 3)]
+    onward += [spread(10, 1, below, 1), spread(11, 2, above, 3)]
+    for one, two in zip(up, down):
+        start([one, two])
     own_copy = pltpu.make_async_copy(piece, out.at[y], out_sem.at[2])
     own_copy.start()
     await_bytes(act_buf.at[0, 0 : NZ - 1], a_send)
@@ -342,12 +347,12 @@
     await_bytes(og_bytes(4), z_send.at[4])
     r_copy.wait_send()
     q_copy.wait_send()
-    for one, two in zip(first, second):
+    for one, two in zip((up[0], down[0], up[1], down[1]), onward):
         one.wait_recv()
         two.start()
-    for copy in rest + second:
+    for copy in up[2:] + down[2:] + onward:
         copy.wait_recv()
-    for copy in first + rest + second:
+    for copy in up + down + onward:
         copy.wait_send()
     for copy in (right_copy, left_copy, own_copy):
         copy.wait()
@@ -396,8 +401,8 @@
             dma,
             dma((5,)),
             dma((5,)),
-            dma((6,)),
-            dma((6,)),
+            dma((12,)),
+            dma((12,)),
             dma((3,)),
         ],
         compiler_params=pltpu.CompilerParams(

time: 64.2 us -> 65.5 us (1.020)
  Pallas kernels: 62.9 us -> 64.1 us
    pallas_call x1, Pallas kernels: 61.5 us -> 62.8 us  [step(): pl.pallas_call(step_kernel, out_shape=(pltpu.VMEM((NY, PIECE, BLK), b16),...]
where the time goes in v2:
time: 65.5 us; the launch traced here: 65.4 us
  Pallas kernels  64.1 us (98%)
  between operations  1.29 us (2%)
    pallas_call x1, Pallas kernels, step(): pl.pallas_call(step_kernel, out_shape=(pltpu.VMEM((NY, PIECE, BLK), b16),...  62.8 us
    pallas_call x1, Pallas kernels, finish(): pl.pallas_call(finish_kernel, out_shape=tuple((jax.ShapeDtypeStruct(a.sha...  1.34 us

profile of v2, /device:TPU:1, one launch (start us, length us, event | category | flops | bytes accessed | tf_op | source)
XLA Modules:
  0.0 65.4 jit_solution(13232440024254492918)
XLA Ops:
  1.3 62.8 %step.1 = (bf16[4,256,512]{2,1,0:T(8,128)(2,1)S(1)}, f32[256,512]{1,0:T(8,128)S(1)}, f32[256,512]{1,0:T(8,128)S(1)}) custom-call(s32[1,1]{1,0:T(1,128)S(6)} %copy.11.fresh, bf16[4,2,16,256]{3,2,1,0:T(8,128)(2,1)} %bitcast.14, bf16[128,16384]{1,0:T(8,128)(2,1)} %og_ref.1, f32[256,512]{1,0:T(8,128)} %bitcast.10, f32[256,512]{1,0:T(8,128)} %bitcast.11, ...), custom_call_target="tpu_custom_call" | custom-call | tf_op jit(solution)/shard_map/step/pallas_call | solution.py:365
  64.1 1.3 %finish.1 = (bf16[4,256,512]{2,1,0:T(8,128)(2,1)}, f32[256,512]{1,0:T(8,128)}, f32[256,512]{1,0:T(8,128)}) custom-call(bf16[4,256,512]{2,1,0:T(8,128)(2,1)S(1)} %get-tuple-element.9.update, f32[256,512]{1,0:T(8,128)S(1)} %get-tuple-element.10.left, f32[256,512]{1,0:T(8,128)S(1)} %get-tuple-element.11.right), custom_call_target="tpu_custom_call" | custom-call | tf_op jit(solution)/shard_map/finish/pallas_call | solution.py:430

commit v3 on v1

v3 whole, which is shorter than its diff:
```python
import jax
import jax.numpy as jnp
from jax import lax
from jax.experimental import pallas as pl
from jax.experimental.pallas import tpu as pltpu
from jax.sharding import PartitionSpec as P

decay_rate = 0.95
epsilon = 1e-06

NZ, NX, NY = 8, 4, 4
BLK = 512
PIECE = 256
TOKENS = 128
ROWS = 32
ORDER = (0, 1, 7, 2, 6, 3, 5, 4)
SLOT = {distance: slot for slot, distance in enumerate(ORDER)}
STAGES = ((0, 0, 8), (1, 0, 8), (2, 0, 8), (3, 0, 4), (3, 4, 8))
VMEM_LIMIT = 56 * 2**20
MESH = pl.DeviceIdType.MESH


def place():
    d = lax.axis_index("dp")
    return d // NX, d % NX, lax.axis_index("mp"), lax.axis_index("helper")


def remote(src, dst, send, recv, device):
    return pltpu.make_async_remote_copy(
        src_ref=src,
        dst_ref=dst,
        send_sem=send,
        recv_sem=recv,
        device_id=device,
        device_id_type=MESH,
    )


def across_rows(a, b):
    return lax.dot_general(a, b, (((0,), (0,)), ((), ())), preferred_element_type=jnp.float32)


def inverse_root(s):
    b16 = jnp.bfloat16
    scale = BLK * jnp.sqrt(jnp.sum(s * s) * (1.0 / (BLK * BLK)) + epsilon)
    first = s * (1.0 / scale)
    first16 = first.astype(b16)
    second = jnp.dot(first16, first16, preferred_element_type=jnp.float32)
    third = jnp.dot(second.astype(b16), first16, preferred_element_type=jnp.float32)
    upper = (250.0 / 4096) * first - (25.0 / 4096) * second + (1.0 / 4096) * third
    high = jnp.dot(third.astype(b16), upper.astype(b16), preferred_element_type=jnp.float32)
    rows = lax.broadcasted_iota(jnp.int32, s.shape, 0)
    columns = lax.broadcasted_iota(jnp.int32, s.shape, 1)
    constant = jnp.where(rows == columns, 25.0 / 16, 0.0)
    low = (-5.0 / 16 - 3125.0 / 4096) * first + (3125.0 / 4096) * second - (1250.0 / 4096) * third
    return ((constant + low + high) * lax.rsqrt(jnp.sqrt(scale))).astype(b16)


def step_kernel(
    fresh,
    act_ref,
    og_ref,
    left_ref,
    right_ref,
    lroot_ref,
    rroot_ref,
    out,
    left_new,
    right_new,
    act_buf,
    act_t,
    og_buf,
    part_out,
    part_in,
    grad_buf,
    stats,
    lroot,
    rroot,
    piece,
    shaped,
    total,
    own_sem,
    z_send,
    z_recv,
    a_send,
    a_recv,
    x_send,
    x_recv,
    y_send,
    y_recv,
    r_send,
    r_recv,
    s_send,
    s_recv,
    u_send,
    u_recv,
    out_sem,
):
    z, x, y, h = place()

    pair = x + 1 - 2 * lax.rem(x, 2)
    partner = NX - 1 - x

    def at(dz, column=x):
        return (lax.rem(z + dz, NZ) * NX + column, y, h)

    def crossed(dz, column=x):
        return (lax.rem(z + dz, NZ) * NX + column, y, 1 - h)

    def at_y(k):
        return (z * NX + x, lax.rem(y + k, NY), h)

    sibling = crossed(0)
    barrier = pltpu.get_barrier_semaphore()
    peers = [crossed(dz) for dz in range(NZ)] + [crossed(dz, pair) for dz in range(NZ)]
    peers += [at(1), at(7), at(0, pair), at(0, partner), at_y(1), at_y(3)]
    for peer in peers:
        pl.semaphore_signal(barrier, inc=1, device_id=peer, device_id_type=MESH)

    def start(copies):
        for copy in copies:
            copy.start()

    def await_bytes(ref, sem):
        pltpu.make_async_copy(ref, ref, sem).wait()

    here = pl.ds(pl.multiple_of(h * PIECE, PIECE), PIECE)

    def target(c):
        owner = pair if c % 2 else x
        return owner, (owner if c >= 2 else NX - 1 - owner)

    def og_part(dz, c):
        column = (lax.rem(z + dz, NZ) * NX + target(c)[1]) * BLK
        return og_ref.at[
            pl.ds(pl.multiple_of(y * ROWS, ROWS), ROWS), pl.ds(pl.multiple_of(column, BLK), BLK)
        ]

    def old_copies():
        return [
            pltpu.make_async_copy(left_ref, stats.at[0, here], own_sem.at[2]),
            pltpu.make_async_copy(right_ref, stats.at[1, here], own_sem.at[3]),
            pltpu.make_async_copy(lroot_ref, lroot.at[here], own_sem.at[4]),
            pltpu.make_async_copy(rroot_ref, rroot, own_sem.at[5]),
            remote(left_ref, stats.at[0, here], s_send.at[0], s_recv.at[0], sibling),
            remote(right_ref, stats.at[1, here], s_send.at[1], s_recv.at[1], sibling),
            remote(lroot_ref, lroot.at[here], s_send.at[2], s_recv.at[2], sibling),
        ]

    def age():
        for copy in old_copies():
            copy.wait()
        stats[...] = decay_rate * stats[...]

    g_copy = remote(grad_buf, grad_buf, s_send.at[3], s_recv.at[3], sibling)
    pl.semaphore_wait(barrier, len(peers))

    @pl.when(h == 0)
    def _():
        start(
            [
                remote(act_ref, act_buf.at[0, SLOT[1], 0], a_send, a_recv.at[0], crossed(1)),
                remote(act_ref, act_buf.at[0, SLOT[7], 0], a_send, a_recv.at[0], crossed(7)),
                remote(act_ref, act_buf.at[0, 0, 0], a_send, a_recv.at[4], sibling),
            ]
        )
        for i, (c, first, end) in enumerate(STAGES):
            for slot in reversed(range(first, end)):
                if slot or c % 2:
                    remote(
                        og_part(ORDER[slot], c),
                        og_buf.at[c, slot, y],
                        z_send,
                        z_recv.at[i],
                        crossed(ORDER[slot], target(c)[0]),
                    ).start()
            if i == 0:
                remote(act_ref, act_buf.at[1, 0, 0], a_send, x_recv, crossed(0, pair)).start()
        start(old_copies())
        age()
        g_copy.wait_recv()

    @pl.when(h == 1)
    def _():
        own_og = [
            pltpu.make_async_copy(og_part(0, c), og_buf.at[c, 0, y], own_sem.at[c * 3])
            for c in (0, 2)
        ]
        own_act = pltpu.make_async_copy(act_ref, act_buf.at[0, 0, 1], own_sem.at[1])

        def send_act(i):
            up, down = act_buf.at[0, SLOT[i]], act_buf.at[0, SLOT[-i % NZ]]
            if i < 4:
                to_up, to_down = act_buf.at[0, SLOT[i + 1]], act_buf.at[0, SLOT[7 - i]]
                if i == 3:
                    up, to_up, down, to_down = up.at[0], to_up.at[0], down.at[1], to_down.at[1]
                if i == 0:
                    up, to_up, down, to_down = act_ref, to_up.at[1], act_ref, to_down.at[1]
                start(
                    [
                        remote(up, to_up, a_send, a_recv.at[i], at(1)),
                        remote(down, to_down, a_send, a_recv.at[i], at(7)),
                    ]
                )
            if i == 0:
                remote(act_ref, act_buf.at[1, 0, 1], x_send, x_recv, at(0, pair)).start()
                return
            for slot in (SLOT[i], SLOT[-i % NZ]) if i < 4 else (SLOT[i],):
                src, dst = act_buf.at[0, slot], act_buf.at[1, slot]
                remote(src, dst, x_send, x_recv, at(0, pair)).start()

        def next_act(i):
            await_bytes(act_buf.at[0, 0:2] if i < 4 else act_buf.at[0, 0], a_recv.at[i - 1])
            send_act(i)

        low, high = lax.rem(y + 3, NY), lax.rem(y + 1, NY)

        def first_y(i):
            c, first, end = STAGES[i]
            if c % 2 == 0:
                own_og[c // 2].wait()
            await_bytes(og_buf.at[c, first if c % 2 else first + 1 : end, 0], z_recv.at[i])
            mine = og_buf.at[c, first:end, y]
            start(
                [
                    remote(mine, mine, y_send, y_recv.at[i, 0], at_y(1)),
                    remote(mine, mine, y_send, y_recv.at[i, 0], at_y(3)),
                ]
            )

        def second_y(i):
            c, first, end = STAGES[i]
            await_bytes(og_buf.at[c, first:end, 0:2], y_recv.at[i, 0])
            middle = (first + end) // 2
            up, down = og_buf.at[c, first:middle, low], og_buf.at[c, middle:end, high]
            start(
                [
                    remote(up, up, y_send, y_recv.at[i, 1], at_y(1)),
                    remote(down, down, y_send, y_recv.at[i, 1], at_y(3)),
                ]
            )

        def turn(bank):
            for half in range(2):
                columns = act_buf[bank, :, half].reshape(NZ * TOKENS, PIECE)
                act_t[bank, pl.ds(half * PIECE, PIECE)] = columns.T

        def product(i):
            c, first, end = STAGES[i]
            await_bytes(og_buf.at[c, first:end, 0], y_recv.at[i, 1])
            rows = og_buf[c, first:end].reshape((end - first) * TOKENS, BLK)
            columns = act_t[c % 2, :, first * TOKENS : end * TOKENS]
            return jnp.dot(columns, rows, preferred_element_type=jnp.float32)

        start(own_og + [own_act])
        send_act(0)
        next_act(1)
        first_y(0)
        next_act(2)
        start(old_copies())
        first_y(1)
        second_y(0)
        next_act(3)
        first_y(2)
        second_y(1)
        own_act.wait()
        await_bytes(act_buf.at[0, 0, 0], a_recv.at[4])
        next_act(4)
        turn(0)
        total[...] = product(0)
        first_y(3)
        second_y(2)
        await_bytes(act_buf.at[1], x_recv)
        turn(1)
        part_out[...] = (total[...] + product(1)).astype(jnp.bfloat16)
        r_copy = remote(part_out, part_in, r_send, r_recv, at(0, partner))
        r_copy.start()
        first_y(4)
        second_y(3)
        total[...] = product(2)
        second_y(4)
        total[...] = total[...] + product(3)
        age()
        r_copy.wait_recv()
        total[...] = total[...] + part_in[...].astype(jnp.float32)
        grad_buf[...] = (total[...] + product(4)).astype(jnp.bfloat16)
        g_copy.start()

    grad = grad_buf[...]
    grad_wide = grad.astype(jnp.float32)
    grad_square = jnp.sum(grad_wide * grad_wide)
    stats[1] = stats[1] + across_rows(grad, grad)
    right_copy = pltpu.make_async_copy(stats.at[1, here], right_new, out_sem.at[0])
    right_copy.start()
    stats[0] = stats[0] + lax.dot_general(
        grad, grad, (((1,), (1,)), ((), ())), preferred_element_type=jnp.float32
    )
    left_copy = pltpu.make_async_copy(stats.at[0, here], left_new, out_sem.at[1])
    left_copy.start()
    renew = fresh[0, 0] > 0
    lroot[...] = jnp.where(renew, inverse_root(stats[0]), lroot[...])
    rroot[...] = jnp.where(renew, inverse_root(stats[1]), rroot[...])
    half = jnp.dot(lroot[...], grad, preferred_element_type=jnp.float32).astype(jnp.bfloat16)
    shaped[...] = jnp.dot(half, rroot[...], preferred_element_type=jnp.float32)
    entries = 1.0 / (BLK * BLK)
    ratio = jnp.sqrt(grad_square * entries + epsilon) / jnp.sqrt(
        jnp.sum(shaped[...] * shaped[...]) * entries + epsilon
    )
    piece[...] = (ratio * shaped[here]).astype(jnp.bfloat16)

    below, above = lax.rem(y + 3, NY), lax.rem(y + 1, NY)
    bottom, top = pl.ds(0, PIECE // 2), pl.ds(PIECE // 2, PIECE // 2)

    def spread(i, rows, owner, k):
        src = piece.at[rows] if owner is y else out.at[owner, rows]
        return remote(src, out.at[owner, rows], u_send.at[i], u_recv.at[i], at_y(k))

    first = [spread(0, bottom, y, 1), spread(1, top, y, 3)]
    rest = [spread(2, top, y, 1), spread(3, bottom, y, 3)]
    second = [spread(4, bottom, below, 1), spread(5, top, above, 3)]
    start(first + rest)
    own_copy = pltpu.make_async_copy(piece, out.at[y], out_sem.at[2])
    own_copy.start()

    @pl.when(h == 0)
    def _():
        await_bytes(act_buf.at[0, 0:2], a_send)
        await_bytes(og_buf.at[0:3, 0:5, 0:2], z_send)

    @pl.when(h == 1)
    def _():
        await_bytes(act_buf.at[0, 0:6], a_send)
        await_bytes(og_buf.at[0:3, 0:5, 0:2], x_send)
        await_bytes(og_buf.at[:, :, 0:3], y_send)
        await_bytes(part_out, r_send)
        g_copy.wait_send()

    for one, two in zip(first, second):
        one.wait_recv()
        two.start()
    for copy in rest + second:
        copy.wait_recv()
    for copy in first + rest + second:
        copy.wait_send()
    for copy in (right_copy, left_copy, own_copy):
        copy.wait()


def step(fresh, act, og, left, right, lroot, rroot):
    hbm = pl.BlockSpec(memory_space=pl.ANY)
    dma = pltpu.SemaphoreType.DMA
    f32, b16 = jnp.float32, jnp.bfloat16
    return pl.pallas_call(
        step_kernel,
        out_shape=(
            pltpu.VMEM((NY, PIECE, BLK), b16),
            pltpu.VMEM((PIECE, BLK), f32),
            pltpu.VMEM((PIECE, BLK), f32),
        ),
        in_specs=[pl.BlockSpec(memory_space=pltpu.SMEM)] + [hbm] * 6,
        out_specs=(hbm,) * 3,
        scratch_shapes=[
            pltpu.VMEM((2, NZ, 2, TOKENS, PIECE), b16),
            pltpu.VMEM((2, BLK, NZ * TOKENS), b16),
            pltpu.VMEM((4, NZ, NY, ROWS, BLK), b16),
            pltpu.VMEM((BLK, BLK), b16),
            pltpu.VMEM((BLK, BLK), b16),
            pltpu.VMEM((BLK, BLK), b16),
            pltpu.VMEM((2, BLK, BLK), f32),
            pltpu.VMEM((BLK, BLK), b16),
            pltpu.VMEM((BLK, BLK), b16),
            pltpu.VMEM((PIECE, BLK), b16),
            pltpu.VMEM((BLK, BLK), f32),
            pltpu.VMEM((BLK, BLK), f32),
            dma((7,)),
            dma,
            dma((5,)),
            dma,
            dma((5,)),
            dma,
            dma,
            dma,
            dma((5, 2)),
            dma,
            dma,
            dma((4,)),
            dma((4,)),
            dma((6,)),
            dma((6,)),
            dma((3,)),
        ],
        compiler_params=pltpu.CompilerParams(
            collective_id=0, has_side_effects=True, vmem_limit_bytes=VMEM_LIMIT
        ),
        name="step",
    )(fresh, act, og, left, right, lroot, rroot)


def finish_kernel(update, left, right, update_out, left_out, right_out, sems):
    copies = [
        pltpu.make_async_copy(update, update_out, sems.at[0]),
        pltpu.make_async_copy(left, left_out, sems.at[1]),
        pltpu.make_async_copy(right, right_out, sems.at[2]),
    ]
    for copy in copies:
        copy.start()
    for copy in copies:
        copy.wait()


def finish(*arrays):
    vmem = pl.BlockSpec(memory_space=pltpu.VMEM)
    anywhere = pl.BlockSpec(memory_space=pl.ANY)
    return pl.pallas_call(
        finish_kernel,
        out_shape=tuple(jax.ShapeDtypeStruct(a.shape, a.dtype) for a in arrays),
        in_specs=[vmem] * 3,
        out_specs=(anywhere,) * 3,
        scratch_shapes=[pltpu.SemaphoreType.DMA((3,))],
        compiler_params=pltpu.CompilerParams(vmem_limit_bytes=4 * 2**20),
        name="finish",
    )(*arrays)


def shards(act, og, left_state, right_state, left_root_old, right_root_old, refresh):
    update, left_new, right_new = finish(
        *step(
            refresh,
            act,
            og,
            left_state[0, 0],
            right_state[0, 0],
            left_root_old[0, 0],
            right_root_old[0, 0],
        )
    )
    return update[:, None], left_new[None, None], right_new[None, None]


def solution(mesh):
    placed = (
        P("dp", ("mp", "helper")),
        P("dp", None),
        P("mp", "dp", "helper", None),
        P("mp", "dp", "helper", None),
        P("mp", "dp", "helper", None),
        P("mp", "dp", None, None),
        P("mp", "dp"),
    )
    return jax.shard_map(
        shards,
        mesh=mesh,
        in_specs=placed,
        out_specs=(
            P(None, "helper", None, "dp"),
            P("mp", "dp", "helper", None),
            P("mp", "dp", "helper", None),
        ),
        check_vma=False,
    )
```

time: 64.2 us -> 62.9 us (0.980); the launches traced: 64.1 us -> 61.8 us
  Pallas kernels: 62.9 us -> 60.5 us
    pallas_call x1, Pallas kernels: 61.5 us -> 59.2 us  [step(): pl.pallas_call(step_kernel, out_shape=(pltpu.VMEM((NY, PIECE, BLK), b16),...]
where the time goes in v3:
time: 62.9 us; the launch traced here: 61.8 us
  Pallas kernels  60.5 us (96%)
  between operations  1.29 us (2%)
    pallas_call x1, Pallas kernels, step(): pl.pallas_call(step_kernel, out_shape=(pltpu.VMEM((NY, PIECE, BLK), b16),...  59.2 us
    pallas_call x1, Pallas kernels, finish(): pl.pallas_call(finish_kernel, out_shape=tuple((jax.ShapeDtypeStruct(a.sha...  1.34 us

profile of v3, /device:TPU:1, one launch (start us, length us, event | category | flops | bytes accessed | tf_op | source)
XLA Modules:
  0.0 61.8 jit_solution(15619310534430722558)
XLA Ops:
  1.3 59.2 %step.1 = (bf16[4,256,512]{2,1,0:T(8,128)(2,1)S(1)}, f32[256,512]{1,0:T(8,128)S(1)}, f32[256,512]{1,0:T(8,128)S(1)}) custom-call(s32[1,1]{1,0:T(1,128)S(6)} %copy.11.fresh, bf16[128,256]{1,0:T(8,128)(2,1)} %act_ref.1, bf16[128,16384]{1,0:T(8,128)(2,1)} %og_ref.1, f32[256,512]{1,0:T(8,128)} %bitcast.9, f32[256,512]{1,0:T(8,128)} %bitcast.10, ...), custom_call_target="tpu_custom_call" | custom-call | tf_op jit(solution)/shard_map/step/pallas_call | solution.py:353
  60.5 1.3 %finish.1 = (bf16[4,256,512]{2,1,0:T(8,128)(2,1)}, f32[256,512]{1,0:T(8,128)}, f32[256,512]{1,0:T(8,128)}) custom-call(bf16[4,256,512]{2,1,0:T(8,128)(2,1)S(1)} %get-tuple-element.9.update, f32[256,512]{1,0:T(8,128)S(1)} %get-tuple-element.10.left, f32[256,512]{1,0:T(8,128)S(1)} %get-tuple-element.11.right), custom_call_target="tpu_custom_call" | custom-call | tf_op jit(solution)/shard_map/finish/pallas_call | solution.py:414

commit v4 on v3

--- a/solution.py
+++ b/solution.py
@@ -67,8 +67,9 @@
     out,
     left_new,
     right_new,
+    act_raw,
+    act_own,
     act_buf,
-    act_t,
     og_buf,
     part_out,
     part_in,
@@ -136,32 +137,35 @@
             pl.ds(pl.multiple_of(y * ROWS, ROWS), ROWS), pl.ds(pl.multiple_of(column, BLK), BLK)
         ]
 
-    def old_copies():
-        return [
-            pltpu.make_async_copy(left_ref, stats.at[0, here], own_sem.at[2]),
-            pltpu.make_async_copy(right_ref, stats.at[1, here], own_sem.at[3]),
-            pltpu.make_async_copy(lroot_ref, lroot.at[here], own_sem.at[4]),
-            pltpu.make_async_copy(rroot_ref, rroot, own_sem.at[5]),
-            remote(left_ref, stats.at[0, here], s_send.at[0], s_recv.at[0], sibling),
-            remote(right_ref, stats.at[1, here], s_send.at[1], s_recv.at[1], sibling),
-            remote(lroot_ref, lroot.at[here], s_send.at[2], s_recv.at[2], sibling),
-        ]
-
-    def age():
-        for copy in old_copies():
-            copy.wait()
-        stats[...] = decay_rate * stats[...]
+    left_in = pltpu.make_async_copy(left_ref, stats.at[0, here], own_sem.at[2])
+    right_in = pltpu.make_async_copy(right_ref, stats.at[1, here], own_sem.at[3])
+    lroot_in = pltpu.make_async_copy(lroot_ref, lroot.at[here], own_sem.at[4])
+    rroot_in = pltpu.make_async_copy(rroot_ref, rroot, own_sem.at[5])
+    left_over = remote(left_ref, stats.at[0, here], s_send.at[0], s_recv.at[0], sibling)
+    right_over = remote(right_ref, stats.at[1, here], s_send.at[1], s_recv.at[1], sibling)
+    lroot_over = remote(lroot_ref, lroot.at[here], s_send.at[2], s_recv.at[2], sibling)
+    rroot_over = remote(rroot, rroot, s_send.at[4], s_recv.at[4], sibling)
+
+    def renew_left(grad):
+        stats[0] = stats[0] + lax.dot_general(
+            grad, grad, (((1,), (1,)), ((), ())), preferred_element_type=jnp.float32
+        )
+        lroot[...] = jnp.where(fresh[0, 0] > 0, inverse_root(stats[0]), lroot[...])
 
     g_copy = remote(grad_buf, grad_buf, s_send.at[3], s_recv.at[3], sibling)
+    raw_in = pltpu.make_async_copy(act_ref, act_raw, own_sem.at[1])
+    raw_in.start()
+    raw_in.wait()
+    act_own[...] = act_raw[...].T
     pl.semaphore_wait(barrier, len(peers))
 
     @pl.when(h == 0)
     def _():
         start(
             [
-                remote(act_ref, act_buf.at[0, SLOT[1], 0], a_send, a_recv.at[0], crossed(1)),
-                remote(act_ref, act_buf.at[0, SLOT[7], 0], a_send, a_recv.at[0], crossed(7)),
-                remote(act_ref, act_buf.at[0, 0, 0], a_send, a_recv.at[4], sibling),
+                remote(act_own, act_buf.at[0, SLOT[1], 0], a_send, a_recv.at[0], crossed(1)),
+                remote(act_own, act_buf.at[0, SLOT[7], 0], a_send, a_recv.at[0], crossed(7)),
+                remote(act_own, act_buf.at[0, 0, 0], a_send, a_recv.at[4], sibling),
             ]
         )
         for i, (c, first, end) in enumerate(STAGES):
@@ -175,10 +179,15 @@
                         crossed(ORDER[slot], target(c)[0]),
                     ).start()
             if i == 0:
-                remote(act_ref, act_buf.at[1, 0, 0], a_send, x_recv, crossed(0, pair)).start()
-        start(old_copies())
-        age()
+                remote(act_own, act_buf.at[1, 0, 0], a_send, x_recv, crossed(0, pair)).start()
+        start([left_in, right_in, lroot_in, left_over, right_over, lroot_over])
+        for copy in (left_in, right_in, lroot_in, left_over, lroot_over):
+            copy.wait()
+        stats[0] = decay_rate * stats[0]
+        stats[1, here] = decay_rate * stats[1, here]
         g_copy.wait_recv()
+        renew_left(grad_buf[...])
+        rroot_over.wait_recv()
 
     @pl.when(h == 1)
     def _():
@@ -186,7 +195,6 @@
             pltpu.make_async_copy(og_part(0, c), og_buf.at[c, 0, y], own_sem.at[c * 3])
             for c in (0, 2)
         ]
-        own_act = pltpu.make_async_copy(act_ref, act_buf.at[0, 0, 1], own_sem.at[1])
 
         def send_act(i):
             up, down = act_buf.at[0, SLOT[i]], act_buf.at[0, SLOT[-i % NZ]]
@@ -195,7 +203,7 @@
                 if i == 3:
                     up, to_up, down, to_down = up.at[0], to_up.at[0], down.at[1], to_down.at[1]
                 if i == 0:
-                    up, to_up, down, to_down = act_ref, to_up.at[1], act_ref, to_down.at[1]
+                    up, to_up, down, to_down = act_own, to_up.at[1], act_own, to_down.at[1]
                 start(
                     [
                         remote(up, to_up, a_send, a_recv.at[i], at(1)),
@@ -203,7 +211,7 @@
                     ]
                 )
             if i == 0:
-                remote(act_ref, act_buf.at[1, 0, 1], x_send, x_recv, at(0, pair)).start()
+                remote(act_own, act_buf.at[1, 0, 1], x_send, x_recv, at(0, pair)).start()
                 return
             for slot in (SLOT[i], SLOT[-i % NZ]) if i < 4 else (SLOT[i],):
                 src, dst = act_buf.at[0, slot], act_buf.at[1, slot]
@@ -240,66 +248,60 @@
                 ]
             )
 
-        def turn(bank):
-            for half in range(2):
-                columns = act_buf[bank, :, half].reshape(NZ * TOKENS, PIECE)
-                act_t[bank, pl.ds(half * PIECE, PIECE)] = columns.T
-
         def product(i):
             c, first, end = STAGES[i]
             await_bytes(og_buf.at[c, first:end, 0], y_recv.at[i, 1])
             rows = og_buf[c, first:end].reshape((end - first) * TOKENS, BLK)
-            columns = act_t[c % 2, :, first * TOKENS : end * TOKENS]
+            blocks = [act_buf[c % 2, slot].reshape(BLK, TOKENS) for slot in range(first, end)]
+            columns = jnp.concatenate(blocks, axis=1)
             return jnp.dot(columns, rows, preferred_element_type=jnp.float32)
 
-        start(own_og + [own_act])
+        start(own_og)
         send_act(0)
+        act_buf[0, 0, 1] = act_own[...]
         next_act(1)
         first_y(0)
         next_act(2)
-        start(old_copies())
+        start([left_in, right_in, lroot_in, rroot_in, left_over, lroot_over])
         first_y(1)
         second_y(0)
         next_act(3)
         first_y(2)
         second_y(1)
-        own_act.wait()
         await_bytes(act_buf.at[0, 0, 0], a_recv.at[4])
         next_act(4)
-        turn(0)
         total[...] = product(0)
         first_y(3)
         second_y(2)
         await_bytes(act_buf.at[1], x_recv)
-        turn(1)
         part_out[...] = (total[...] + product(1)).astype(jnp.bfloat16)
         r_copy = remote(part_out, part_in, r_send, r_recv, at(0, partner))
         r_copy.start()
+        for copy in (left_in, right_in, lroot_in, rroot_in, left_over, lroot_over):
+            copy.wait()
+        right_over.wait_recv()
+        stats[...] = decay_rate * stats[...]
         first_y(4)
         second_y(3)
         total[...] = product(2)
         second_y(4)
         total[...] = total[...] + product(3)
-        age()
         r_copy.wait_recv()
         total[...] = total[...] + part_in[...].astype(jnp.float32)
         grad_buf[...] = (total[...] + product(4)).astype(jnp.bfloat16)
         g_copy.start()
+        grad = grad_buf[...]
+        stats[1] = stats[1] + across_rows(grad, grad)
+        rroot[...] = jnp.where(fresh[0, 0] > 0, inverse_root(stats[1]), rroot[...])
+        rroot_over.start()
+        renew_left(grad)
 
     grad = grad_buf[...]
     grad_wide = grad.astype(jnp.float32)
     grad_square = jnp.sum(grad_wide * grad_wide)
-    stats[1] = stats[1] + across_rows(grad, grad)
     right_copy = pltpu.make_async_copy(stats.at[1, here], right_new, out_sem.at[0])
-    right_copy.start()
-    stats[0] = stats[0] + lax.dot_general(
-        grad, grad, (((1,), (1,)), ((), ())), preferred_element_type=jnp.float32
-    )
     left_copy = pltpu.make_async_copy(stats.at[0, here], left_new, out_sem.at[1])
     left_copy.start()
-    renew = fresh[0, 0] > 0
-    lroot[...] = jnp.where(renew, inverse_root(stats[0]), lroot[...])
-    rroot[...] = jnp.where(renew, inverse_root(stats[1]), rroot[...])
     half = jnp.dot(lroot[...], grad, preferred_element_type=jnp.float32).astype(jnp.bfloat16)
     shaped[...] = jnp.dot(half, rroot[...], preferred_element_type=jnp.float32)
     entries = 1.0 / (BLK * BLK)
@@ -324,11 +326,16 @@
 
     @pl.when(h == 0)
     def _():
+        stats[1, here] = stats[1, here] + across_rows(grad_buf[:, 0:PIECE], grad_buf[...])
+        right_copy.start()
+        right_over.wait_send()
         await_bytes(act_buf.at[0, 0:2], a_send)
         await_bytes(og_buf.at[0:3, 0:5, 0:2], z_send)
 
     @pl.when(h == 1)
     def _():
+        right_copy.start()
+        rroot_over.wait_send()
         await_bytes(act_buf.at[0, 0:6], a_send)
         await_bytes(og_buf.at[0:3, 0:5, 0:2], x_send)
         await_bytes(og_buf.at[:, :, 0:3], y_send)
@@ -360,8 +367,9 @@
         in_specs=[pl.BlockSpec(memory_space=pltpu.SMEM)] + [hbm] * 6,
         out_specs=(hbm,) * 3,
         scratch_shapes=[
-            pltpu.VMEM((2, NZ, 2, TOKENS, PIECE), b16),
-            pltpu.VMEM((2, BLK, NZ * TOKENS), b16),
+            pltpu.VMEM((TOKENS, PIECE), b16),
+            pltpu.VMEM((PIECE, TOKENS), b16),
+            pltpu.VMEM((2, NZ, 2, PIECE, TOKENS), b16),
             pltpu.VMEM((4, NZ, NY, ROWS, BLK), b16),
             pltpu.VMEM((BLK, BLK), b16),
             pltpu.VMEM((BLK, BLK), b16),
@@ -383,8 +391,8 @@
             dma((5, 2)),
             dma,
             dma,
-            dma((4,)),
-            dma((4,)),
+            dma((5,)),
+            dma((5,)),
             dma((6,)),
             dma((6,)),
             dma((3,)),

time: 62.9 us -> 63.9 us (1.016); the launches traced: 61.8 us -> 63.8 us
  Pallas kernels: 60.5 us -> 62.5 us
    pallas_call x1, Pallas kernels: 59.2 us -> 61.1 us  [step(): pl.pallas_call(step_kernel, out_shape=(pltpu.VMEM((NY, PIECE, BLK), b16),...]
where the time goes in v4:
time: 63.9 us; the launch traced here: 63.8 us
  Pallas kernels  62.5 us (98%)
  between operations  1.29 us (2%)
    pallas_call x1, Pallas kernels, step(): pl.pallas_call(step_kernel, out_shape=(pltpu.VMEM((NY, PIECE, BLK), b16),...  61.1 us
    pallas_call x1, Pallas kernels, finish(): pl.pallas_call(finish_kernel, out_shape=tuple((jax.ShapeDtypeStruct(a.sha...  1.34 us

profile of v4, /device:TPU:1, one launch (start us, length us, event | category | flops | bytes accessed | tf_op | source)
XLA Modules:
  0.0 63.8 jit_solution(13025763857597719449)
XLA Ops:
  1.3 61.1 %step.1 = (bf16[4,256,512]{2,1,0:T(8,128)(2,1)S(1)}, f32[256,512]{1,0:T(8,128)S(1)}, f32[256,512]{1,0:T(8,128)S(1)}) custom-call(s32[1,1]{1,0:T(1,128)S(6)} %copy.11.fresh, bf16[128,256]{1,0:T(8,128)(2,1)} %act_ref.1, bf16[128,16384]{1,0:T(8,128)(2,1)} %og_ref.1, f32[256,512]{1,0:T(8,128)} %bitcast.9, f32[256,512]{1,0:T(8,128)} %bitcast.10, ...), custom_call_target="tpu_custom_call" | custom-call | tf_op jit(solution)/shard_map/step/pallas_call | solution.py:360
  62.4 1.3 %finish.1 = (bf16[4,256,512]{2,1,0:T(8,128)(2,1)}, f32[256,512]{1,0:T(8,128)}, f32[256,512]{1,0:T(8,128)}) custom-call(bf16[4,256,512]{2,1,0:T(8,128)(2,1)S(1)} %get-tuple-element.9.update, f32[256,512]{1,0:T(8,128)S(1)} %get-tuple-element.10.left, f32[256,512]{1,0:T(8,128)S(1)} %get-tuple-element.11.right), custom_call_target="tpu_custom_call" | custom-call | tf_op jit(solution)/shard_map/finish/pallas_call | solution.py:422

commit v5 on v4

--- a/solution.py
+++ b/solution.py
@@ -15,6 +15,7 @@
 ROWS = 32
 ORDER = (0, 1, 7, 2, 6, 3, 5, 4)
 SLOT = {distance: slot for slot, distance in enumerate(ORDER)}
+REACH = {1: 5, -1: 2}
 STAGES = ((0, 0, 8), (1, 0, 8), (2, 0, 8), (3, 0, 4), (3, 4, 8))
 VMEM_LIMIT = 56 * 2**20
 MESH = pl.DeviceIdType.MESH
@@ -155,19 +156,10 @@
     g_copy = remote(grad_buf, grad_buf, s_send.at[3], s_recv.at[3], sibling)
     raw_in = pltpu.make_async_copy(act_ref, act_raw, own_sem.at[1])
     raw_in.start()
-    raw_in.wait()
-    act_own[...] = act_raw[...].T
     pl.semaphore_wait(barrier, len(peers))
 
     @pl.when(h == 0)
     def _():
-        start(
-            [
-                remote(act_own, act_buf.at[0, SLOT[1], 0], a_send, a_recv.at[0], crossed(1)),
-                remote(act_own, act_buf.at[0, SLOT[7], 0], a_send, a_recv.at[0], crossed(7)),
-                remote(act_own, act_buf.at[0, 0, 0], a_send, a_recv.at[4], sibling),
-            ]
-        )
         for i, (c, first, end) in enumerate(STAGES):
             for slot in reversed(range(first, end)):
                 if slot or c % 2:
@@ -179,7 +171,16 @@
                         crossed(ORDER[slot], target(c)[0]),
                     ).start()
             if i == 0:
-                remote(act_own, act_buf.at[1, 0, 0], a_send, x_recv, crossed(0, pair)).start()
+                raw_in.wait()
+                act_own[...] = act_raw[...].T
+                start(
+                    [
+                        remote(act_own, act_buf.at[0, SLOT[1], 0], a_send, a_recv.at[0], crossed(1)),
+                        remote(act_own, act_buf.at[0, SLOT[7], 0], a_send, a_recv.at[0], crossed(7)),
+                        remote(act_own, act_buf.at[0, 0, 0], a_send, a_recv.at[5], sibling),
+                        remote(act_own, act_buf.at[1, 0, 0], a_send, x_recv, crossed(0, pair)),
+                    ]
+                )
         start([left_in, right_in, lroot_in, left_over, right_over, lroot_over])
         for copy in (left_in, right_in, lroot_in, left_over, lroot_over):
             copy.wait()
@@ -197,28 +198,26 @@
         ]
 
         def send_act(i):
-            up, down = act_buf.at[0, SLOT[i]], act_buf.at[0, SLOT[-i % NZ]]
-            if i < 4:
-                to_up, to_down = act_buf.at[0, SLOT[i + 1]], act_buf.at[0, SLOT[7 - i]]
-                if i == 3:
-                    up, to_up, down, to_down = up.at[0], to_up.at[0], down.at[1], to_down.at[1]
-                if i == 0:
-                    up, to_up, down, to_down = act_own, to_up.at[1], act_own, to_down.at[1]
-                start(
-                    [
-                        remote(up, to_up, a_send, a_recv.at[i], at(1)),
-                        remote(down, to_down, a_send, a_recv.at[i], at(7)),
-                    ]
-                )
+            source = act_own if i == 0 else None
+            for way in (1, -1):
+                distance = way * i
+                if i < REACH[way]:
+                    src = source if i == 0 else act_buf.at[0, SLOT[distance % NZ]]
+                    dst = act_buf.at[0, SLOT[(distance + way) % NZ]]
+                    if i == 0:
+                        dst = dst.at[1]
+                    remote(src, dst, a_send, a_recv.at[i], at(way % NZ)).start()
+                if 0 < i <= REACH[way]:
+                    slot = SLOT[distance % NZ]
+                    remote(
+                        act_buf.at[0, slot], act_buf.at[1, slot], x_send, x_recv, at(0, pair)
+                    ).start()
             if i == 0:
                 remote(act_own, act_buf.at[1, 0, 1], x_send, x_recv, at(0, pair)).start()
-                return
-            for slot in (SLOT[i], SLOT[-i % NZ]) if i < 4 else (SLOT[i],):
-                src, dst = act_buf.at[0, slot], act_buf.at[1, slot]
-                remote(src, dst, x_send, x_recv, at(0, pair)).start()
 
         def next_act(i):
-            await_bytes(act_buf.at[0, 0:2] if i < 4 else act_buf.at[0, 0], a_recv.at[i - 1])
+            chunks = sum(i <= reach for reach in REACH.values())
+            await_bytes(act_buf.at[0, 0:chunks], a_recv.at[i - 1])
             send_act(i)
 
         low, high = lax.rem(y + 3, NY), lax.rem(y + 1, NY)
@@ -257,6 +256,8 @@
             return jnp.dot(columns, rows, preferred_element_type=jnp.float32)
 
         start(own_og)
+        raw_in.wait()
+        act_own[...] = act_raw[...].T
         send_act(0)
         act_buf[0, 0, 1] = act_own[...]
         next_act(1)
@@ -268,10 +269,11 @@
         next_act(3)
         first_y(2)
         second_y(1)
-        await_bytes(act_buf.at[0, 0, 0], a_recv.at[4])
+        await_bytes(act_buf.at[0, 0, 0], a_recv.at[5])
         next_act(4)
+        first_y(3)
+        next_act(5)
         total[...] = product(0)
-        first_y(3)
         second_y(2)
         await_bytes(act_buf.at[1], x_recv)
         part_out[...] = (total[...] + product(1)).astype(jnp.bfloat16)
@@ -384,7 +386,7 @@
             dma,
             dma((5,)),
             dma,
-            dma((5,)),
+            dma((6,)),
             dma,
             dma,
             dma,

time: 63.9 us -> 66.6 us (1.042)
  Pallas kernels: 62.5 us -> 65.2 us
    pallas_call x1, Pallas kernels: 61.1 us -> 63.9 us  [step(): pl.pallas_call(step_kernel, out_shape=(pltpu.VMEM((NY, PIECE, BLK), b16),...]
where the time goes in v5:
time: 66.6 us; the launch traced here: 66.5 us
  Pallas kernels  65.2 us (98%)
  between operations  1.29 us (2%)
    pallas_call x1, Pallas kernels, step(): pl.pallas_call(step_kernel, out_shape=(pltpu.VMEM((NY, PIECE, BLK), b16),...  63.9 us
    pallas_call x1, Pallas kernels, finish(): pl.pallas_call(finish_kernel, out_shape=tuple((jax.ShapeDtypeStruct(a.sha...  1.34 us

profile of v5, /device:TPU:1, one launch (start us, length us, event | category | flops | bytes accessed | tf_op | source)
XLA Modules:
  0.0 66.5 jit_solution(7878453853065701362)
XLA Ops:
  1.3 63.9 %step.1 = (bf16[4,256,512]{2,1,0:T(8,128)(2,1)S(1)}, f32[256,512]{1,0:T(8,128)S(1)}, f32[256,512]{1,0:T(8,128)S(1)}) custom-call(s32[1,1]{1,0:T(1,128)S(6)} %copy.11.fresh, bf16[128,256]{1,0:T(8,128)(2,1)} %act_ref.1, bf16[128,16384]{1,0:T(8,128)(2,1)} %og_ref.1, f32[256,512]{1,0:T(8,128)} %bitcast.9, f32[256,512]{1,0:T(8,128)} %bitcast.10, ...), custom_call_target="tpu_custom_call" | custom-call | tf_op jit(solution)/shard_map/step/pallas_call | solution.py:362
  65.1 1.3 %finish.1 = (bf16[4,256,512]{2,1,0:T(8,128)(2,1)}, f32[256,512]{1,0:T(8,128)}, f32[256,512]{1,0:T(8,128)}) custom-call(bf16[4,256,512]{2,1,0:T(8,128)(2,1)S(1)} %get-tuple-element.9.update, f32[256,512]{1,0:T(8,128)S(1)} %get-tuple-element.10.left, f32[256,512]{1,0:T(8,128)S(1)} %get-tuple-element.11.right), custom_call_target="tpu_custom_call" | custom-call | tf_op jit(solution)/shard_map/finish/pallas_call | solution.py:424

commit v6 on v4

--- a/solution.py
+++ b/solution.py
@@ -15,6 +15,7 @@
 ROWS = 32
 ORDER = (0, 1, 7, 2, 6, 3, 5, 4)
 SLOT = {distance: slot for slot, distance in enumerate(ORDER)}
+NEAR = (1, 7, 2, 6)
 STAGES = ((0, 0, 8), (1, 0, 8), (2, 0, 8), (3, 0, 4), (3, 4, 8))
 VMEM_LIMIT = 56 * 2**20
 MESH = pl.DeviceIdType.MESH
@@ -111,10 +112,12 @@
     def at_y(k):
         return (z * NX + x, lax.rem(y + k, NY), h)
 
+    raw_in = pltpu.make_async_copy(act_ref, act_raw, own_sem.at[1])
+    raw_in.start()
     sibling = crossed(0)
     barrier = pltpu.get_barrier_semaphore()
     peers = [crossed(dz) for dz in range(NZ)] + [crossed(dz, pair) for dz in range(NZ)]
-    peers += [at(1), at(7), at(0, pair), at(0, partner), at_y(1), at_y(3)]
+    peers += [at(dz) for dz in NEAR] + [at(0, pair), at(0, partner), at_y(1), at_y(3)]
     for peer in peers:
         pl.semaphore_signal(barrier, inc=1, device_id=peer, device_id_type=MESH)
 
@@ -153,21 +156,17 @@
         lroot[...] = jnp.where(fresh[0, 0] > 0, inverse_root(stats[0]), lroot[...])
 
     g_copy = remote(grad_buf, grad_buf, s_send.at[3], s_recv.at[3], sibling)
-    raw_in = pltpu.make_async_copy(act_ref, act_raw, own_sem.at[1])
-    raw_in.start()
     raw_in.wait()
     act_own[...] = act_raw[...].T
     pl.semaphore_wait(barrier, len(peers))
 
     @pl.when(h == 0)
     def _():
-        start(
-            [
-                remote(act_own, act_buf.at[0, SLOT[1], 0], a_send, a_recv.at[0], crossed(1)),
-                remote(act_own, act_buf.at[0, SLOT[7], 0], a_send, a_recv.at[0], crossed(7)),
-                remote(act_own, act_buf.at[0, 0, 0], a_send, a_recv.at[4], sibling),
-            ]
-        )
+        for dz in NEAR:
+            dst = act_buf.at[0, SLOT[dz], 0]
+            remote(act_own, dst, a_send, a_recv.at[0], crossed(dz)).start()
+        remote(act_own, act_buf.at[0, 0, 0], a_send, a_recv.at[2], sibling).start()
+        remote(act_own, act_buf.at[1, 0, 0], a_send, x_recv, crossed(0, pair)).start()
         for i, (c, first, end) in enumerate(STAGES):
             for slot in reversed(range(first, end)):
                 if slot or c % 2:
@@ -178,8 +177,6 @@
                         z_recv.at[i],
                         crossed(ORDER[slot], target(c)[0]),
                     ).start()
-            if i == 0:
-                remote(act_own, act_buf.at[1, 0, 0], a_send, x_recv, crossed(0, pair)).start()
         start([left_in, right_in, lroot_in, left_over, right_over, lroot_over])
         for copy in (left_in, right_in, lroot_in, left_over, lroot_over):
             copy.wait()
@@ -196,30 +193,22 @@
             for c in (0, 2)
         ]
 
-        def send_act(i):
-            up, down = act_buf.at[0, SLOT[i]], act_buf.at[0, SLOT[-i % NZ]]
-            if i < 4:
-                to_up, to_down = act_buf.at[0, SLOT[i + 1]], act_buf.at[0, SLOT[7 - i]]
-                if i == 3:
-                    up, to_up, down, to_down = up.at[0], to_up.at[0], down.at[1], to_down.at[1]
-                if i == 0:
-                    up, to_up, down, to_down = act_own, to_up.at[1], act_own, to_down.at[1]
-                start(
-                    [
-                        remote(up, to_up, a_send, a_recv.at[i], at(1)),
-                        remote(down, to_down, a_send, a_recv.at[i], at(7)),
-                    ]
-                )
-            if i == 0:
-                remote(act_own, act_buf.at[1, 0, 1], x_send, x_recv, at(0, pair)).start()
-                return
-            for slot in (SLOT[i], SLOT[-i % NZ]) if i < 4 else (SLOT[i],):
+        def exchange(distances):
+            for distance in distances:
+                slot = SLOT[distance]
                 src, dst = act_buf.at[0, slot], act_buf.at[1, slot]
                 remote(src, dst, x_send, x_recv, at(0, pair)).start()
 
-        def next_act(i):
-            await_bytes(act_buf.at[0, 0:2] if i < 4 else act_buf.at[0, 0], a_recv.at[i - 1])
-            send_act(i)
+        def pass_act():
+            await_bytes(act_buf.at[0, 0:4], a_recv.at[0])
+            for distance, half in ((2, 0), (6, 1)):
+                way = distance // 2 if distance == 2 else 7
+                chunk = act_buf.at[0, SLOT[distance]]
+                middle = act_buf.at[0, SLOT[4], half]
+                beyond = act_buf.at[0, SLOT[3 if distance == 2 else 5]]
+                remote(chunk.at[half], middle, a_send, a_recv.at[1], at(distance)).start()
+                remote(chunk, beyond, a_send, a_recv.at[1], at(way)).start()
+            exchange(NEAR)
 
         low, high = lax.rem(y + 3, NY), lax.rem(y + 1, NY)
 
@@ -256,20 +245,22 @@
             columns = jnp.concatenate(blocks, axis=1)
             return jnp.dot(columns, rows, preferred_element_type=jnp.float32)
 
+        for dz in NEAR:
+            dst = act_buf.at[0, SLOT[dz], 1]
+            remote(act_own, dst, a_send, a_recv.at[0], at(dz)).start()
+        remote(act_own, act_buf.at[1, 0, 1], x_send, x_recv, at(0, pair)).start()
         start(own_og)
-        send_act(0)
         act_buf[0, 0, 1] = act_own[...]
-        next_act(1)
+        pass_act()
+        start([left_in, right_in, lroot_in, rroot_in, left_over, lroot_over])
         first_y(0)
-        next_act(2)
-        start([left_in, right_in, lroot_in, rroot_in, left_over, lroot_over])
         first_y(1)
         second_y(0)
-        next_act(3)
+        await_bytes(act_buf.at[0, 0:3], a_recv.at[1])
+        exchange((3, 5, 4))
         first_y(2)
         second_y(1)
-        await_bytes(act_buf.at[0, 0, 0], a_recv.at[4])
-        next_act(4)
+        await_bytes(act_buf.at[0, 0, 0], a_recv.at[2])
         total[...] = product(0)
         first_y(3)
         second_y(2)
@@ -329,14 +320,14 @@
         stats[1, here] = stats[1, here] + across_rows(grad_buf[:, 0:PIECE], grad_buf[...])
         right_copy.start()
         right_over.wait_send()
-        await_bytes(act_buf.at[0, 0:2], a_send)
+        await_bytes(act_buf.at[0, 0:3], a_send)
         await_bytes(og_buf.at[0:3, 0:5, 0:2], z_send)
 
     @pl.when(h == 1)
     def _():
         right_copy.start()
         rroot_over.wait_send()
-        await_bytes(act_buf.at[0, 0:6], a_send)
+        await_bytes(og_buf.at[0, 0:5, 0:4], a_send)
         await_bytes(og_buf.at[0:3, 0:5, 0:2], x_send)
         await_bytes(og_buf.at[:, :, 0:3], y_send)
         await_bytes(part_out, r_send)

time: 63.9 us -> 64.5 us (level)
  no operation moved by 1% of the time
where the time goes in v6:
time: 64.5 us; the launch traced here: 64.3 us
  Pallas kernels  63 us (98%)
  between operations  1.29 us (2%)
    pallas_call x1, Pallas kernels, step(): pl.pallas_call(step_kernel, out_shape=(pltpu.VMEM((NY, PIECE, BLK), b16),...  61.7 us
    pallas_call x1, Pallas kernels, finish(): pl.pallas_call(finish_kernel, out_shape=tuple((jax.ShapeDtypeStruct(a.sha...  1.34 us

profile of v6, /device:TPU:1, one launch (start us, length us, event | category | flops | bytes accessed | tf_op | source)
XLA Modules:
  0.0 64.3 jit_solution(1011744759927263734)
XLA Ops:
  1.3 61.7 %step.1 = (bf16[4,256,512]{2,1,0:T(8,128)(2,1)S(1)}, f32[256,512]{1,0:T(8,128)S(1)}, f32[256,512]{1,0:T(8,128)S(1)}) custom-call(s32[1,1]{1,0:T(1,128)S(6)} %copy.11.fresh, bf16[128,256]{1,0:T(8,128)(2,1)} %act_ref.1, bf16[128,16384]{1,0:T(8,128)(2,1)} %og_ref.1, f32[256,512]{1,0:T(8,128)} %bitcast.9, f32[256,512]{1,0:T(8,128)} %bitcast.10, ...), custom_call_target="tpu_custom_call" | custom-call | tf_op jit(solution)/shard_map/step/pallas_call | solution.py:351
  63.0 1.3 %finish.1 = (bf16[4,256,512]{2,1,0:T(8,128)(2,1)}, f32[256,512]{1,0:T(8,128)}, f32[256,512]{1,0:T(8,128)}) custom-call(bf16[4,256,512]{2,1,0:T(8,128)(2,1)S(1)} %get-tuple-element.9.update, f32[256,512]{1,0:T(8,128)S(1)} %get-tuple-element.10.left, f32[256,512]{1,0:T(8,128)S(1)} %get-tuple-element.11.right), custom_call_target="tpu_custom_call" | custom-call | tf_op jit(solution)/shard_map/finish/pallas_call | solution.py:413

commit v7 on v4

--- a/solution.py
+++ b/solution.py
@@ -67,9 +67,8 @@
     out,
     left_new,
     right_new,
-    act_raw,
-    act_own,
     act_buf,
+    act_t,
     og_buf,
     part_out,
     part_in,
@@ -153,19 +152,15 @@
         lroot[...] = jnp.where(fresh[0, 0] > 0, inverse_root(stats[0]), lroot[...])
 
     g_copy = remote(grad_buf, grad_buf, s_send.at[3], s_recv.at[3], sibling)
-    raw_in = pltpu.make_async_copy(act_ref, act_raw, own_sem.at[1])
-    raw_in.start()
-    raw_in.wait()
-    act_own[...] = act_raw[...].T
     pl.semaphore_wait(barrier, len(peers))
 
     @pl.when(h == 0)
     def _():
         start(
             [
-                remote(act_own, act_buf.at[0, SLOT[1], 0], a_send, a_recv.at[0], crossed(1)),
-                remote(act_own, act_buf.at[0, SLOT[7], 0], a_send, a_recv.at[0], crossed(7)),
-                remote(act_own, act_buf.at[0, 0, 0], a_send, a_recv.at[4], sibling),
+                remote(act_ref, act_buf.at[0, SLOT[1], 0], a_send, a_recv.at[0], crossed(1)),
+                remote(act_ref, act_buf.at[0, SLOT[7], 0], a_send, a_recv.at[0], crossed(7)),
+                remote(act_ref, act_buf.at[0, 0, 0], a_send, a_recv.at[4], sibling),
             ]
         )
         for i, (c, first, end) in enumerate(STAGES):
@@ -179,7 +174,7 @@
                         crossed(ORDER[slot], target(c)[0]),
                     ).start()
             if i == 0:
-                remote(act_own, act_buf.at[1, 0, 0], a_send, x_recv, crossed(0, pair)).start()
+                remote(act_ref, act_buf.at[1, 0, 0], a_send, x_recv, crossed(0, pair)).start()
         start([left_in, right_in, lroot_in, left_over, right_over, lroot_over])
         for copy in (left_in, right_in, lroot_in, left_over, lroot_over):
             copy.wait()
@@ -195,6 +190,7 @@
             pltpu.make_async_copy(og_part(0, c), og_buf.at[c, 0, y], own_sem.at[c * 3])
             for c in (0, 2)
         ]
+        own_act = pltpu.make_async_copy(act_ref, act_buf.at[0, 0, 1], own_sem.at[1])
 
         def send_act(i):
             up, down = act_buf.at[0, SLOT[i]], act_buf.at[0, SLOT[-i % NZ]]
@@ -203,7 +199,7 @@
                 if i == 3:
                     up, to_up, down, to_down = up.at[0], to_up.at[0], down.at[1], to_down.at[1]
                 if i == 0:
-                    up, to_up, down, to_down = act_own, to_up.at[1], act_own, to_down.at[1]
+                    up, to_up, down, to_down = act_ref, to_up.at[1], act_ref, to_down.at[1]
                 start(
                     [
                         remote(up, to_up, a_send, a_recv.at[i], at(1)),
@@ -211,7 +207,7 @@
                     ]
                 )
             if i == 0:
-                remote(act_own, act_buf.at[1, 0, 1], x_send, x_recv, at(0, pair)).start()
+                remote(act_ref, act_buf.at[1, 0, 1], x_send, x_recv, at(0, pair)).start()
                 return
             for slot in (SLOT[i], SLOT[-i % NZ]) if i < 4 else (SLOT[i],):
                 src, dst = act_buf.at[0, slot], act_buf.at[1, slot]
@@ -248,17 +244,20 @@
                 ]
             )
 
+        def turn(bank):
+            for half in range(2):
+                columns = act_buf[bank, :, half].reshape(NZ * TOKENS, PIECE)
+                act_t[bank, pl.ds(half * PIECE, PIECE)] = columns.T
+
         def product(i):
             c, first, end = STAGES[i]
             await_bytes(og_buf.at[c, first:end, 0], y_recv.at[i, 1])
             rows = og_buf[c, first:end].reshape((end - first) * TOKENS, BLK)
-            blocks = [act_buf[c % 2, slot].reshape(BLK, TOKENS) for slot in range(first, end)]
-            columns = jnp.concatenate(blocks, axis=1)
+            columns = act_t[c % 2, :, first * TOKENS : end * TOKENS]
             return jnp.dot(columns, rows, preferred_element_type=jnp.float32)
 
-        start(own_og)
+        start(own_og + [own_act])
         send_act(0)
-        act_buf[0, 0, 1] = act_own[...]
         next_act(1)
         first_y(0)
         next_act(2)
@@ -268,24 +267,27 @@
         next_act(3)
         first_y(2)
         second_y(1)
+        own_act.wait()
         await_bytes(act_buf.at[0, 0, 0], a_recv.at[4])
         next_act(4)
+        turn(0)
         total[...] = product(0)
         first_y(3)
         second_y(2)
         await_bytes(act_buf.at[1], x_recv)
+        turn(1)
         part_out[...] = (total[...] + product(1)).astype(jnp.bfloat16)
         r_copy = remote(part_out, part_in, r_send, r_recv, at(0, partner))
         r_copy.start()
-        for copy in (left_in, right_in, lroot_in, rroot_in, left_over, lroot_over):
-            copy.wait()
-        right_over.wait_recv()
-        stats[...] = decay_rate * stats[...]
         first_y(4)
         second_y(3)
         total[...] = product(2)
         second_y(4)
         total[...] = total[...] + product(3)
+        for copy in (left_in, right_in, lroot_in, rroot_in, left_over, lroot_over):
+            copy.wait()
+        right_over.wait_recv()
+        stats[...] = decay_rate * stats[...]
         r_copy.wait_recv()
         total[...] = total[...] + part_in[...].astype(jnp.float32)
         grad_buf[...] = (total[...] + product(4)).astype(jnp.bfloat16)
@@ -367,9 +369,8 @@
         in_specs=[pl.BlockSpec(memory_space=pltpu.SMEM)] + [hbm] * 6,
         out_specs=(hbm,) * 3,
         scratch_shapes=[
-            pltpu.VMEM((TOKENS, PIECE), b16),
-            pltpu.VMEM((PIECE, TOKENS), b16),
-            pltpu.VMEM((2, NZ, 2, PIECE, TOKENS), b16),
+            pltpu.VMEM((2, NZ, 2, TOKENS, PIECE), b16),
+            pltpu.VMEM((2, BLK, NZ * TOKENS), b16),
             pltpu.VMEM((4, NZ, NY, ROWS, BLK), b16),
             pltpu.VMEM((BLK, BLK), b16),
             pltpu.VMEM((BLK, BLK), b16),

time: 63.9 us -> 64.5 us (level)
  no operation moved by 1% of the time
where the time goes in v7:
time: 64.5 us; the launch traced here: 64.4 us
  Pallas kernels  63.1 us (98%)
  between operations  1.29 us (2%)
    pallas_call x1, Pallas kernels, step(): pl.pallas_call(step_kernel, out_shape=(pltpu.VMEM((NY, PIECE, BLK), b16),...  61.7 us
    pallas_call x1, Pallas kernels, finish(): pl.pallas_call(finish_kernel, out_shape=tuple((jax.ShapeDtypeStruct(a.sha...  1.34 us

profile of v7, /device:TPU:1, one launch (start us, length us, event | category | flops | bytes accessed | tf_op | source)
XLA Modules:
  0.0 64.4 jit_solution(3221554883183277884)
XLA Ops:
  1.3 61.7 %step.1 = (bf16[4,256,512]{2,1,0:T(8,128)(2,1)S(1)}, f32[256,512]{1,0:T(8,128)S(1)}, f32[256,512]{1,0:T(8,128)S(1)}) custom-call(s32[1,1]{1,0:T(1,128)S(6)} %copy.11.fresh, bf16[128,256]{1,0:T(8,128)(2,1)} %act_ref.1, bf16[128,16384]{1,0:T(8,128)(2,1)} %og_ref.1, f32[256,512]{1,0:T(8,128)} %bitcast.9, f32[256,512]{1,0:T(8,128)} %bitcast.10, ...), custom_call_target="tpu_custom_call" | custom-call | tf_op jit(solution)/shard_map/step/pallas_call | solution.py:362
  63.0 1.3 %finish.1 = (bf16[4,256,512]{2,1,0:T(8,128)(2,1)}, f32[256,512]{1,0:T(8,128)}, f32[256,512]{1,0:T(8,128)}) custom-call(bf16[4,256,512]{2,1,0:T(8,128)(2,1)S(1)} %get-tuple-element.9.update, f32[256,512]{1,0:T(8,128)S(1)} %get-tuple-element.10.left, f32[256,512]{1,0:T(8,128)S(1)} %get-tuple-element.11.right), custom_call_target="tpu_custom_call" | custom-call | tf_op jit(solution)/shard_map/finish/pallas_call | solution.py:423

commit v8 on v3

--- a/solution.py
+++ b/solution.py
@@ -150,7 +150,6 @@
     def age():
         for copy in old_copies():
             copy.wait()
-        stats[...] = decay_rate * stats[...]
 
     g_copy = remote(grad_buf, grad_buf, s_send.at[3], s_recv.at[3], sibling)
     pl.semaphore_wait(barrier, len(peers))
@@ -289,10 +288,10 @@
     grad = grad_buf[...]
     grad_wide = grad.astype(jnp.float32)
     grad_square = jnp.sum(grad_wide * grad_wide)
-    stats[1] = stats[1] + across_rows(grad, grad)
+    stats[1] = decay_rate * stats[1] + across_rows(grad, grad)
     right_copy = pltpu.make_async_copy(stats.at[1, here], right_new, out_sem.at[0])
     right_copy.start()
-    stats[0] = stats[0] + lax.dot_general(
+    stats[0] = decay_rate * stats[0] + lax.dot_general(
         grad, grad, (((1,), (1,)), ((), ())), preferred_element_type=jnp.float32
     )
     left_copy = pltpu.make_async_copy(stats.at[0, here], left_new, out_sem.at[1])

time: 62.9 us -> 62.9 us (level)
  no operation moved by 1% of the time
where the time goes in v8:
time: 62.9 us; the launch traced here: 61.8 us
  Pallas kernels  60.5 us (96%)
  between operations  1.29 us (2%)
    pallas_call x1, Pallas kernels, step(): pl.pallas_call(step_kernel, out_shape=(pltpu.VMEM((NY, PIECE, BLK), b16),...  59.2 us
    pallas_call x1, Pallas kernels, finish(): pl.pallas_call(finish_kernel, out_shape=tuple((jax.ShapeDtypeStruct(a.sha...  1.34 us

profile of v8, /device:TPU:1, one launch (start us, length us, event | category | flops | bytes accessed | tf_op | source)
XLA Modules:
  0.0 61.8 jit_solution(12003031851636681478)
XLA Ops:
  1.3 59.2 %step.1 = (bf16[4,256,512]{2,1,0:T(8,128)(2,1)S(1)}, f32[256,512]{1,0:T(8,128)S(1)}, f32[256,512]{1,0:T(8,128)S(1)}) custom-call(s32[1,1]{1,0:T(1,128)S(6)} %copy.11.fresh, bf16[128,256]{1,0:T(8,128)(2,1)} %act_ref.1, bf16[128,16384]{1,0:T(8,128)(2,1)} %og_ref.1, f32[256,512]{1,0:T(8,128)} %bitcast.9, f32[256,512]{1,0:T(8,128)} %bitcast.10, ...), custom_call_target="tpu_custom_call" | custom-call | tf_op jit(solution)/shard_map/step/pallas_call | solution.py:352
  60.5 1.3 %finish.1 = (bf16[4,256,512]{2,1,0:T(8,128)(2,1)}, f32[256,512]{1,0:T(8,128)}, f32[256,512]{1,0:T(8,128)}) custom-call(bf16[4,256,512]{2,1,0:T(8,128)(2,1)S(1)} %get-tuple-element.9.update, f32[256,512]{1,0:T(8,128)S(1)} %get-tuple-element.10.left, f32[256,512]{1,0:T(8,128)S(1)} %get-tuple-element.11.right), custom_call_target="tpu_custom_call" | custom-call | tf_op jit(solution)/shard_map/finish/pallas_call | solution.py:413
